TPU v7x, 32 devices: a whole 2x2x4 slice. The times are simulated.
32 devices in a mesh: groups: 2 (over x), expert: 16 (over z, y, core), cuts: 1.
Axes of the slice: x: 2, y: 2, z: 4, core: 2. Of those that a mesh axis runs over, the one named last changes fastest.
Arguments:
- quant: bfloat16 [512, 3584], P(('groups', 'expert', 'cuts')), parts along dimension 0, may hold values from -6 to 6
- scales: bfloat16 [512, 28], P(('groups', 'expert', 'cuts')), parts along dimension 0, may hold values from 0.29882812 to 3
- routes: int32 [512, 8], P(('groups', 'expert', 'cuts')), parts along dimension 0, may hold values from 0 to 15, all different within a row; in each aligned block of 16 rows (0 to 15, 16 to 31, ...) at most 12 rows name the same one
- gates: float32 [512, 8], P(('groups', 'expert', 'cuts')), parts along dimension 0, may hold values from 0.05 to 0.25
- cotangent: bfloat16 [512, 3584], P(('groups', 'expert', 'cuts')), parts along dimension 0, may hold values from -1.5 to 1.5
- w_gate: bfloat16 [16, 3584, 1280], P('expert', None, 'cuts'), may hold values from -0.09375 to 0.09375
- w_up: bfloat16 [16, 3584, 1280], P('expert', None, 'cuts'), may hold values from -0.09375 to 0.09375
- w_down: bfloat16 [16, 1280, 3584], P('expert', 'cuts'), may hold values from -0.15625 to 0.15625
Outputs:
- mixed: bfloat16 [512, 3584], P(('groups', 'expert', 'cuts')), parts along dimension 0
- grad_tokens: bfloat16 [512, 3584], P(('groups', 'expert', 'cuts')), parts along dimension 0
- grad_gates: float32 [512, 8], P(('groups', 'expert', 'cuts')), parts along dimension 0
- grad_up: bfloat16 [32, 3584, 1280], P(('groups', 'expert'), None, 'cuts'), parts along dimension 0
- grad_down: bfloat16 [32, 1280, 3584], P(('groups', 'expert'), 'cuts'), parts along dimension 0
There are 2 independent parts, one for each index of `groups`. A program takes and returns all parts, laid end to end along the dimension named above; an argument that names none is the same for every part. Nothing has to cross between parts.
Inputs may be any that keep to these rules, and one draw needn't show every extreme that they name: `routes`: each row names 8 different experts. Within the 16 rows of one device no expert is named by more than 12 rows, and in some device's rows some expert is named by exactly 12.
All inputs are finite; a program needn't handle non-finite values.
Results may differ from a plain program's by a relative error of at most 0.0072.
Values may be sent and summed in bfloat16 or wider, within the bound.
A program may use at most 128 MiB of HBM per device.

v0:
```python
import jax
import jax.numpy as jnp
from jax import lax
from jax.sharding import PartitionSpec as P


def expert_pass(inputs, row_grad, weight_gate, weight_up, weight_down):
    gate_pre = jnp.dot(inputs, weight_gate, preferred_element_type=jnp.float32)
    up_pre = jnp.dot(inputs, weight_up, preferred_element_type=jnp.float32)
    gate_sig = jax.nn.sigmoid(gate_pre)
    activated = gate_pre * gate_sig
    hidden = (activated * up_pre).astype(jnp.bfloat16)
    output_part = jnp.dot(hidden, weight_down, preferred_element_type=jnp.float32)
    down_grad = lax.dot_general(
        hidden, row_grad, (((0,), (0,)), ((), ())), preferred_element_type=jnp.float32
    )
    hidden_grad = lax.dot_general(
        row_grad, weight_down, (((1,), (1,)), ((), ())), preferred_element_type=jnp.float32
    )
    gate_grad = (hidden_grad * up_pre * gate_sig * (1.0 + gate_pre * (1.0 - gate_sig))).astype(
        jnp.bfloat16
    )
    up_grad = (hidden_grad * activated).astype(jnp.bfloat16)
    up_weight_grad = lax.dot_general(
        inputs, up_grad, (((0,), (0,)), ((), ())), preferred_element_type=jnp.float32
    )
    input_part = lax.dot_general(
        gate_grad, weight_gate, (((1,), (1,)), ((), ())), preferred_element_type=jnp.float32
    )
    input_part = input_part + lax.dot_general(
        up_grad, weight_up, (((1,), (1,)), ((), ())), preferred_element_type=jnp.float32
    )
    return (output_part, input_part, down_grad, up_weight_grad)


def run_expert(quant_rows, scale_rows, grad_rows, w_gate, w_up, w_down):
    width = quant_rows.shape[-1]
    blocks = scale_rows.shape[-1]
    quant_flat = quant_rows.reshape(-1, width)
    row_count = quant_flat.shape[0]
    scale_flat = scale_rows.reshape(row_count, blocks)
    inputs = (
        (
            quant_flat.astype(jnp.float32).reshape(row_count, blocks, width // blocks)
            * scale_flat.astype(jnp.float32)[:, :, None]
        )
        .reshape(row_count, width)
        .astype(jnp.bfloat16)
    )
    return expert_pass(inputs, grad_rows.reshape(row_count, width), w_gate[0], w_up[0], w_down[0])


def duplicate(array, copies):
    spread_shape = (array.shape[0], copies) + array.shape[1:]
    return jnp.broadcast_to(array[:, None], spread_shape).reshape(
        (array.shape[0] * copies,) + array.shape[1:]
    )


def place_rows(placement, rows):
    return jnp.einsum("est,td->esd", placement, rows, preferred_element_type=jnp.float32).astype(
        jnp.bfloat16
    )


def local(quant, scales, routes, gates, cotangent, w_gate, w_up, w_down):
    expert_count = lax.axis_size("expert")
    cut_count = lax.axis_size("cuts")
    token_count = quant.shape[0]
    width = quant.shape[1]
    top_count = routes.shape[1]
    capacity = min(token_count, 3 * token_count * top_count // (2 * expert_count))
    expert_ids = lax.broadcasted_iota(jnp.int32, (1, 1, expert_count), 2)
    onehot = (routes[:, :, None] == expert_ids).astype(jnp.float32)
    assigned = jnp.sum(onehot, 1)
    weight_of = jnp.sum(gates[:, :, None] * onehot, 1)
    slot_of = jnp.cumsum(assigned, 0) - assigned
    slot_ids = lax.broadcasted_iota(jnp.int32, (1, capacity, 1), 1).astype(jnp.float32)
    placement = assigned.T[:, None, :] * (slot_of.T[:, None, :] == slot_ids).astype(jnp.float32)
    placement_b = placement.astype(jnp.bfloat16)
    quant_send = place_rows(placement_b, quant)
    scale_send = place_rows(placement_b, scales)
    cot_slot = place_rows(placement_b, cotangent)
    cot_float = cot_slot.astype(jnp.float32)
    gate_slot = jnp.sum(placement * weight_of.T[:, None, :], -1)
    grad_send = (gate_slot[:, :, None] * cot_float).astype(jnp.bfloat16)
    quant_rows, scale_rows, grad_rows = (
        lax.all_to_all(
            duplicate(quant_send, cut_count),
            ("expert", "cuts"),
            split_axis=0,
            concat_axis=0,
            tiled=True,
        ),
        lax.all_to_all(
            duplicate(scale_send, cut_count),
            ("expert", "cuts"),
            split_axis=0,
            concat_axis=0,
            tiled=True,
        ),
        lax.all_to_all(
            duplicate(grad_send, cut_count),
            ("expert", "cuts"),
            split_axis=0,
            concat_axis=0,
            tiled=True,
        ),
    )
    output_part, input_part, down_grad, up_weight_grad = run_expert(
        quant_rows, scale_rows, grad_rows, w_gate, w_up, w_down
    )
    shape_back = (expert_count * cut_count, capacity, width)
    output_parts, input_parts = (
        lax.all_to_all(
            output_part.reshape(shape_back),
            ("expert", "cuts"),
            split_axis=0,
            concat_axis=0,
            tiled=True,
        ),
        lax.all_to_all(
            input_part.reshape(shape_back),
            ("expert", "cuts"),
            split_axis=0,
            concat_axis=0,
            tiled=True,
        ),
    )
    output_back = jnp.sum(output_parts.reshape(expert_count, cut_count, capacity, width), 1).astype(
        jnp.bfloat16
    )
    input_back = jnp.sum(input_parts.reshape(expert_count, cut_count, capacity, width), 1).astype(
        jnp.bfloat16
    )
    output_float = output_back.astype(jnp.float32)
    weighted = placement * weight_of.T[:, None, :]
    mixed = jnp.einsum(
        "est,esd->td",
        weighted,
        output_float,
        precision=lax.Precision.HIGHEST,
        preferred_element_type=jnp.float32,
    ).astype(jnp.bfloat16)
    grad_tokens = jnp.einsum(
        "est,esd->td",
        placement,
        input_back.astype(jnp.float32),
        precision=lax.Precision.HIGHEST,
        preferred_element_type=jnp.float32,
    ).astype(jnp.bfloat16)
    projected = jnp.sum(cot_float * output_float, -1)
    per_pair = jnp.sum(placement * projected[:, :, None], 1)
    grad_gates = jnp.sum(onehot * per_pair.T[:, None, :], -1)
    return (
        mixed,
        grad_tokens,
        grad_gates,
        up_weight_grad.astype(jnp.bfloat16)[None],
        down_grad.astype(jnp.bfloat16)[None],
    )


def solution(mesh):
    in_specs = (
        P(("groups", "expert", "cuts"), None),
        P(("groups", "expert", "cuts"), None),
        P(("groups", "expert", "cuts"), None),
        P(("groups", "expert", "cuts"), None),
        P(("groups", "expert", "cuts"), None),
        P("expert", None, "cuts"),
        P("expert", None, "cuts"),
        P("expert", "cuts", None),
    )
    out_specs = (
        P(("groups", "expert", "cuts"), None),
        P(("groups", "expert", "cuts"), None),
        P(("groups", "expert", "cuts"), None),
        P(("groups", "expert"), None, "cuts"),
        P(("groups", "expert"), "cuts", None),
    )
    return jax.shard_map(local, mesh=mesh, in_specs=in_specs, out_specs=out_specs, check_vma=False)
```

profile of v0, /device:TPU:15, one launch (start us, length us, event | category | flops | bytes accessed | tf_op | source)
XLA Modules:
  0.0 250.6 jit_solution(1873719389113957671)
XLA Ops:
  0.6 0.0 copy-start
  0.7 0.8 copy.43
  1.5 0.8 copy.44
  2.2 0.1 select_reduce_fusion.1
  2.4 0.9 convolution_convert_fusion.4
  3.3 0.7 reshape.88
  4.1 6.6 %all-to-all-start.1 = ((bf16[16,2,168]{2,1,0:T(2,128)(2,1)}), bf16[16,2,168]{2,1,0:T(2,128)(2,1)S(1)}, u32[]{:S(2)}, u32[]{:S(2)}) async-start(bf16[16,2,168]{2,1,0:T(2,128)(2,1)} %reshape.88), calls=%async_computation.1 | async-start | bytes 32768 | tf_op jit(solution)/shard_map/all_to_all | solution.py:95
  10.6 1.5 convolution_convert_fusion.3
  12.2 2.0 copy.46
  14.2 0.6 all-to-all-done.1
  14.7 6.0 %all-to-all-start = ((bf16[16,12,3584]{2,1,0:T(8,128)(2,1)}), bf16[16,12,3584]{2,1,0:T(8,128)(2,1)S(1)}, u32[]{:S(2)}, u32[]{:S(2)}) async-start(bf16[16,12,3584]{2,1,0:T(8,128)(2,1)} %copy.46), calls=%async_computation | async-start | bytes 3670016 | tf_op jit(solution)/shard_map/all_to_all | solution.py:88
  20.8 0.1 reshape.89
  20.9 41.7 %all-to-all-done = bf16[16,12,3584]{2,1,0:T(8,128)(2,1)S(1)} async-done(((bf16[16,12,3584]{2,1,0:T(8,128)(2,1)}), bf16[16,12,3584]{2,1,0:T(8,128)(2,1)S(1)}, u32[]{:S(2)}, u32[]{:S(2)}) %all-to-all-start) | async-done | bytes 1376288 | tf_op jit(solution)/shard_map/all_to_all | solution.py:88
  62.6 0.0 copy-start.2
  62.6 2.3 reshape.79
  64.8 0.0 slice-start
  64.8 2.5 %multiply_convert_fusion = bf16[192,28,128]{2,1,0:T(8,128)(2,1)S(1)} fusion(f32[192,28,128]{2,1,0:T(8,128)} %reshape.79, f32[192,28]{1,0:T(8,128)S(1)} %reshape.80), kind=kLoop, calls=%fused_computation.24 | loop fusion | flops 1376256 | bytes 4150272 | tf_op jit(solution)/shard_map/convert_element_type | solution.py:48
  67.4 0.0 copy-done.2
  67.4 0.0 slice-start.1
  67.4 0.0 slice-start.2
  67.4 5.9 %fusion.12 = f32[192,1280]{1,0:T(8,128)S(1)} fusion(bf16[1,3584,1280]{2,1,0:T(8,128)(2,1)} %param.13, bf16[24,8,28,128]{3,2,1,0:T(8,128)(2,1)S(1)} %bitcast.76), kind=kOutput, calls=%fused_computation.14 | convolution fusion | flops 1761607680 | bytes 11534336 | tf_op jit(solution)/shard_map/dot_general | solution.py:8
  73.3 0.0 slice-done
  73.3 0.0 slice-done.1
  73.3 0.0 slice-done.2
  73.3 0.0 copy-start.6
  73.3 3.1 %multiply_convert_fusion.4 = (bf16[192,1280]{1,0:T(8,128)(2,1)S(1)}, f32[192,1280]{1,0:T(8,128)}) fusion(f32[192,1280]{1,0:T(8,128)S(1)} %fusion.12, bf16[1,3584,1280]{2,1,0:T(8,128)(2,1)S(1)} %bitcast.73, bf16[24,8,28,128]{3,2,1,0:T(8,128)(2,1)S(1)} %bitcast.77), kind=kOutput, calls=%fused_computation.38 | convolution fusion | flops 1763082240 | bytes 13008896 | tf_op jit(solution)/shard_map/dot_general | solution.py:9
  76.4 0.0 copy-done.6
  76.4 0.1 dot_general.45
  76.6 6.1 %fusion.2 = bf16[16,12,3584]{2,1,0:T(8,128)(2,1)S(1)} fusion(bf16[16,12,1280]{2,1,0:T(8,128)(2,1)S(1)} %dot_general.45, bf16[1,1280,3584]{2,1,0:T(8,128)(2,1)} %param.15), kind=kOutput, calls=%fused_computation.4 | convolution fusion | flops 1761607680 | bytes 11042816 | tf_op jit(solution)/shard_map/dot_general | solution.py:13
  82.7 46.4 %all_to_all.25 = bf16[16,12,3584]{2,1,0:T(8,128)(2,1)S(1)} all-to-all(bf16[16,12,3584]{2,1,0:T(8,128)(2,1)S(1)} %fusion.2), channel_id=1, replica_groups=mesh['groups'=2,'expert'=16,'cuts'=1] {'expert','cuts'}, dimensions={0} | all-to-all | bytes 2752512 | tf_op jit(solution)/shard_map/all_to_all | solution.py:115
  129.1 0.0 copy-start.3
  129.1 1.2 copy-done.3
  130.3 0.0 copy-done
  130.3 1.1 multiply_reduce_fusion
  131.4 0.1 fusion.33
  131.6 0.3 multiply_convert_fusion.1
  131.9 0.8 copy.53
  132.6 46.6 %all_to_all.26 = bf16[16,12,3584]{2,1,0:T(8,128)(2,1)S(1)} all-to-all(bf16[16,12,3584]{2,1,0:T(8,128)(2,1)S(1)} %copy.53), channel_id=1, replica_groups=mesh['groups'=2,'expert'=16,'cuts'=1] {'expert','cuts'}, dimensions={0} | all-to-all | bytes 2752512 | tf_op jit(solution)/shard_map/all_to_all | solution.py:102
  179.2 1.3 reshape.77
  180.5 7.4 %multiply_convert_fusion.2 = (bf16[192,1280]{1,0:T(8,128)(2,1)S(1)}, f32[192,1280]{1,0:T(8,128)S(1)}) fusion(f32[192,1280]{1,0:T(8,128)} %copy-done.6, bf16[192,3584]{1,0:T(8,128)(2,1)} %reshape.77, bf16[1,1280,3584]{2,1,0:T(8,128)(2,1)} %param.15), kind=kOutput, calls=%fused_computation.36 | convolution fusion | flops 1763082240 | bytes 13008896 | tf_op jit(solution)/shard_map/dot_general | solution.py:17
  187.9 0.0 copy-start.4
  187.9 0.0 slice-done.3
  187.9 0.0 slice-done.4
  188.0 0.0 slice-done.5
  188.0 0.0 copy-start.7
  188.0 0.0 copy-start.8
  188.0 3.1 %fusion.6 = f32[192,3584]{1,0:T(8,128)S(1)} fusion(bf16[192,1280]{1,0:T(8,128)(2,1)S(1)} %get-tuple-element.18, bf16[1,3584,1280]{2,1,0:T(8,128)(2,1)S(1)} %bitcast.75), kind=kOutput, calls=%fused_computation.8 | convolution fusion | flops 1761607680 | bytes 12419072 | tf_op jit(solution)/shard_map/dot_general | solution.py:30
  191.1 0.0 copy-done.4
  191.1 0.0 copy-done.7
  191.1 0.0 copy-done.8
  191.1 6.8 %fusion.14 = bf16[192,3584]{1,0:T(8,128)(2,1)S(1)} fusion(f32[192,3584]{1,0:T(8,128)S(1)} %fusion.6, bf16[1,3584,1280]{2,1,0:T(8,128)(2,1)} %param.13, f32[192,1280]{1,0:T(8,128)S(1)} %copy-done.7, f32[192,1280]{1,0:T(8,128)S(1)} %get-tuple-element.19, f32[192,1280]{1,0:T(8,128)S(1)} %copy-done.8), kind=kOutput, calls=%fused_computation.16 | convolution fusion | flops 1765441536 | bytes 16252928 | tf_op jit(solution)/shard_map/dot_general | solution.py:27
  197.9 1.4 reshape.78
  199.4 5.3 %all-to-all-start.4 = ((bf16[16,12,3584]{2,1,0:T(8,128)(2,1)}), bf16[16,12,3584]{2,1,0:T(8,128)(2,1)}, u32[]{:S(2)}, u32[]{:S(2)}) async-start(bf16[16,12,3584]{2,1,0:T(8,128)(2,1)} %reshape.78), calls=%async_computation.4 | async-start | bytes 3670016 | tf_op jit(solution)/shard_map/all_to_all | solution.py:122
  204.7 2.3 reshape.81
  207.0 0.2 select_reduce_fusion
  207.2 0.7 copy.55
  207.9 4.0 %fusion.18 = bf16[16,3584]{1,0:T(8,128)(2,1)} fusion(bf16[16,12,3584]{2,1,0:T(8,128)(2,1)} %copy-done.3, f32[16,16]{0,1:T(8,128)S(1)} %bitcast.86, f32[16,16]{0,1:T(8,128)S(1)} %bitcast.82, f32[16,16]{0,1:T(8,128)S(1)} %bitcast_subtract_fusion, f32[12]{0:T(128)S(1)} %iota_convert_fusion), kind=kOutput, calls=%fused_computation.22 | convolution fusion | flops 132187136 | bytes 1494064 | tf_op jit(solution)/shard_map/est,esd->td/dot_general | solution.py:138
  211.9 7.6 %fusion.1 = bf16[1,1280,3584]{2,1,0:T(8,128)(2,1)} fusion(bf16[192,1280]{1,0:T(8,128)(2,1)S(1)} %get-tuple-element.14, bf16[192,3584]{1,0:T(8,128)(2,1)} %reshape.77), kind=kOutput, calls=%fused_computation.3 | convolution fusion | flops 1766195200 | bytes 11042816 | tf_op jit(solution)/shard_map/dot_general | solution.py:14
  219.5 0.9 mul.106
  220.3 0.2 copy-done.5
  220.5 7.8 %fusion = bf16[1,3584,1280]{2,1,0:T(8,128)(2,1)} fusion(bf16[192,1280]{1,0:T(8,128)(2,1)S(1)} %copy-done.5, f32[192,3584]{1,0:T(8,128)S(1)} %reshape.81, f32[24,8,28,128]{3,2,1,0:T(8,128)S(1)} %bitcast.71), kind=kOutput, calls=%fused_computation.2 | convolution fusion | flops 1767571456 | bytes 15171584 | tf_op jit(solution)/shard_map/dot_general | solution.py:24
  228.3 18.3 %all-to-all-done.4 = bf16[16,12,3584]{2,1,0:T(8,128)(2,1)} async-done(((bf16[16,12,3584]{2,1,0:T(8,128)(2,1)}), bf16[16,12,3584]{2,1,0:T(8,128)(2,1)}, u32[]{:S(2)}, u32[]{:S(2)}) %all-to-all-start.4) | async-done | bytes 1376288 | tf_op jit(solution)/shard_map/all_to_all | solution.py:122
  246.6 4.0 %fusion.19 = bf16[16,3584]{1,0:T(8,128)(2,1)} fusion(bf16[16,12,3584]{2,1,0:T(8,128)(2,1)} %all-to-all-done.4, f32[16,16]{0,1:T(8,128)S(1)} %bitcast.83, f32[16,16]{0,1:T(8,128)S(1)} %bitcast_subtract_fusion, f32[12]{0:T(128)S(1)} %iota_convert_fusion), kind=kOutput, calls=%fused_computation.23 | convolution fusion | flops 132184064 | bytes 1493040 | tf_op jit(solution)/shard_map/est,esd->td/dot_general | solution.py:145
  250.6 0.0 copy-done.1
  (12 shorter events, 0.1 us)
Async XLA Ops:
  0.6 129.7 %copy-start = (bf16[16,3584]{1,0:T(8,128)(2,1)S(1)}, bf16[16,3584]{1,0:T(8,128)(2,1)}, u32[]{:S(2)}) copy-start(bf16[16,3584]{1,0:T(8,128)(2,1)} %param.12) | copy-start | bytes 344068
  4.1 10.7 %all-to-all-start.1 = ((bf16[16,2,168]{2,1,0:T(2,128)(2,1)}), bf16[16,2,168]{2,1,0:T(2,128)(2,1)S(1)}, u32[]{:S(2)}, u32[]{:S(2)}) async-start(bf16[16,2,168]{2,1,0:T(2,128)(2,1)} %reshape.88), calls=%async_computation.1 | async-start | bytes 32768 | tf_op jit(solution)/shard_map/all_to_all | solution.py:95
  14.7 47.8 %all-to-all-start = ((bf16[16,12,3584]{2,1,0:T(8,128)(2,1)}), bf16[16,12,3584]{2,1,0:T(8,128)(2,1)S(1)}, u32[]{:S(2)}, u32[]{:S(2)}) async-start(bf16[16,12,3584]{2,1,0:T(8,128)(2,1)} %copy.46), calls=%async_computation | async-start | bytes 3670016 | tf_op jit(solution)/shard_map/all_to_all | solution.py:88
  62.6 4.8 %copy-start.2 = (bf16[16,12,3584]{2,1,0:T(8,128)(2,1)}, bf16[16,12,3584]{2,1,0:T(8,128)(2,1)S(1)}, u32[]{:S(2)}) copy-start(bf16[16,12,3584]{2,1,0:T(8,128)(2,1)S(1)} %all-to-all-done) | copy-start | bytes 4128772
  64.8 8.4 %slice-start = ((s8[9175040]{0:T(1024)(128)(4,1)}), s8[4194304]{0:T(1024)(128)(4,1)S(1)}, s32[]{:S(2)}) async-start(s8[9175040]{0:T(1024)(128)(4,1)} %bitcast.72), calls=%async_computation.5 | async-start | bytes 8388608
  67.4 5.9 %slice-start.1 = ((s8[9175040]{0:T(1024)(128)(4,1)}), s8[4194304]{0:T(1024)(128)(4,1)S(1)}, s32[]{:S(2)}) async-start(s8[9175040]{0:T(1024)(128)(4,1)} %bitcast.72), calls=%async_computation.6 | async-start | bytes 8388608
  67.4 5.9 %slice-start.2 = ((s8[9175040]{0:T(1024)(128)(4,1)}), s8[786432]{0:T(1024)(128)(4,1)S(1)}, s32[]{:S(2)}) async-start(s8[9175040]{0:T(1024)(128)(4,1)} %bitcast.72), calls=%async_computation.7 | async-start | bytes 1572864
  73.3 3.1 %copy-start.6 = (f32[192,1280]{1,0:T(8,128)}, f32[192,1280]{1,0:T(8,128)S(1)}, u32[]{:S(2)}) copy-start(f32[192,1280]{1,0:T(8,128)S(1)} %fusion.12) | copy-start | bytes 2949124
  129.1 1.2 copy-start.3
  179.2 8.7 %slice-start.3 = ((s8[9175040]{0:T(1024)(128)(4,1)}), s8[786432]{0:T(1024)(128)(4,1)S(1)}, s32[]{:S(2)}) async-start(s8[9175040]{0:T(1024)(128)(4,1)} %bitcast.74), calls=%async_computation.8 | async-start | bytes 1572864
  180.5 7.5 %slice-start.4 = ((s8[9175040]{0:T(1024)(128)(4,1)}), s8[4194304]{0:T(1024)(128)(4,1)S(1)}, s32[]{:S(2)}) async-start(s8[9175040]{0:T(1024)(128)(4,1)} %bitcast.74), calls=%async_computation.9 | async-start | bytes 8388608
  180.5 7.5 %slice-start.5 = ((s8[9175040]{0:T(1024)(128)(4,1)}), s8[4194304]{0:T(1024)(128)(4,1)S(1)}, s32[]{:S(2)}) async-start(s8[9175040]{0:T(1024)(128)(4,1)} %bitcast.74), calls=%async_computation.10 | async-start | bytes 8388608
  187.9 3.2 %copy-start.4 = (bf16[192,1280]{1,0:T(8,128)(2,1)}, bf16[192,1280]{1,0:T(8,128)(2,1)S(1)}, u32[]{:S(2)}) copy-start(bf16[192,1280]{1,0:T(8,128)(2,1)S(1)} %get-tuple-element.18) | copy-start | bytes 1474564
  188.0 3.1 %copy-start.7 = (f32[192,1280]{1,0:T(8,128)S(1)}, f32[192,1280]{1,0:T(8,128)}, u32[]{:S(2)}) copy-start(f32[192,1280]{1,0:T(8,128)} %copy-done.6) | copy-start | bytes 2949124
  188.0 3.1 %copy-start.8 = (f32[192,1280]{1,0:T(8,128)S(1)}, f32[192,1280]{1,0:T(8,128)}, u32[]{:S(2)}) copy-start(f32[192,1280]{1,0:T(8,128)} %get-tuple-element.15) | copy-start | bytes 2949124
  199.4 47.3 %all-to-all-start.4 = ((bf16[16,12,3584]{2,1,0:T(8,128)(2,1)}), bf16[16,12,3584]{2,1,0:T(8,128)(2,1)}, u32[]{:S(2)}, u32[]{:S(2)}) async-start(bf16[16,12,3584]{2,1,0:T(8,128)(2,1)} %reshape.78), calls=%async_computation.4 | async-start | bytes 3670016 | tf_op jit(solution)/shard_map/all_to_all | solution.py:122
  219.5 1.0 copy-start.5
  220.5 30.1 %copy-start.1 = (bf16[16,3584]{1,0:T(8,128)(2,1)S(1)}, bf16[16,3584]{1,0:T(8,128)(2,1)}, u32[]{:S(2)}) copy-start(bf16[16,3584]{1,0:T(8,128)(2,1)} %param.12) | copy-start | bytes 344068
where the time goes:
time: 251 us
  blocking collectives  92.9 us (37%)
  waiting for transfers between devices  60.6 us (24%)
  matrix products  59.4 us (24%)
  starting transfers between devices  17.9 us (7%)
  local copies, waits for them, and re-layouts  15.6 us (6%)
  other arithmetic  3.24 us (1%)
    all_to_all x1, blocking collectives, local(): lax.all_to_all(duplicate(grad_send, cut_count), ('expert', 'cuts'), split...  46.6 us
    all_to_all x1, blocking collectives, local(): lax.all_to_all(output_part.reshape(shape_back), ('expert', 'cuts'), split...  46.4 us
    all_to_all x1, waiting for transfers between devices, local(): lax.all_to_all(duplicate(quant_send, cut_count), ('expert', 'cuts'), spli...  41.7 us
    all_to_all x1, waiting for transfers between devices, local(): lax.all_to_all(input_part.reshape(shape_back), ('expert', 'cuts'), split_...  18.3 us
    dot_general x1, matrix products, expert_pass(): lax.dot_general(inputs, up_grad, (((0,), (0,)), ((), ())), preferred_elem...  7.78 us
    dot_general x1, matrix products, expert_pass(): lax.dot_general(hidden, row_grad, (((0,), (0,)), ((), ())), preferred_ele...  7.59 us
    dot_general x1, matrix products, expert_pass(): lax.dot_general(row_grad, weight_down, (((1,), (1,)), ((), ())), preferre...  7.44 us
    dot_general x1, matrix products, expert_pass(): lax.dot_general(gate_grad, weight_gate, (((1,), (1,)), ((), ())), preferr...  6.79 us
  transfers between devices with their start and end apart: 3, of which 3 were waited for; matrix products, arithmetic and copies ran while one was open for 11% of the time, Pallas kernels for 0%

commit v1 on v0

v1 whole, which is shorter than its diff:
```python
import jax
import jax.numpy as jnp
from jax import lax
from jax.sharding import PartitionSpec as P

AXES = ("expert", "cuts")


def local(quant, scales, routes, gates, cotangent, w_gate, w_up, w_down):
    cut_count = lax.axis_size("cuts")
    expert_count = lax.axis_size("expert")
    me = lax.axis_index("expert") * cut_count + lax.axis_index("cuts")
    count, width = quant.shape
    blocks = scales.shape[1]
    inputs = (
        (
            quant.astype(jnp.float32).reshape(count, blocks, width // blocks)
            * scales.astype(jnp.float32)[:, :, None]
        )
        .reshape(count, width)
        .astype(jnp.bfloat16)
    )
    expert_ids = lax.broadcasted_iota(jnp.int32, (1, 1, expert_count), 2)
    onehot = (routes[:, :, None] == expert_ids).astype(jnp.float32)
    weight_of = jnp.sum(gates[:, :, None] * onehot, 1)
    x_all = lax.all_gather(inputs, AXES, axis=0, tiled=True)
    weight_all = lax.all_gather(weight_of, AXES, axis=0, tiled=True)
    cot_all = lax.all_gather(cotangent, AXES, axis=0, tiled=True)
    mine = lax.broadcasted_iota(jnp.int32, (1, expert_count), 1) == lax.axis_index("expert")
    weight = jnp.sum(jnp.where(mine, weight_all, 0.0), 1, keepdims=True)
    cot_float = cot_all.astype(jnp.float32)
    row_grad = (weight * cot_float).astype(jnp.bfloat16)

    wg, wu, wd = w_gate[0], w_up[0], w_down[0]
    gate_pre = jnp.dot(x_all, wg, preferred_element_type=jnp.float32)
    up_pre = jnp.dot(x_all, wu, preferred_element_type=jnp.float32)
    sig = jax.nn.sigmoid(gate_pre)
    act = gate_pre * sig
    hidden = (act * up_pre).astype(jnp.bfloat16)
    out = jnp.dot(hidden, wd, preferred_element_type=jnp.float32)
    dots = jnp.sum(cot_float * out, 1, keepdims=True)
    mixed = lax.psum_scatter(
        (weight * out).astype(jnp.bfloat16), AXES, scatter_dimension=0, tiled=True
    )
    dots_home = lax.psum_scatter(
        jnp.where(mine, dots, 0.0), AXES, scatter_dimension=0, tiled=True
    )
    nt = (((1,), (1,)), ((), ()))
    tn = (((0,), (0,)), ((), ()))
    hidden_grad = lax.dot_general(row_grad, wd, nt, preferred_element_type=jnp.float32)
    gate_grad = (hidden_grad * up_pre * sig * (1.0 + gate_pre * (1.0 - sig))).astype(jnp.bfloat16)
    up_grad = (hidden_grad * act).astype(jnp.bfloat16)
    dx = lax.dot_general(gate_grad, wg, nt, preferred_element_type=jnp.float32)
    dx = dx + lax.dot_general(up_grad, wu, nt, preferred_element_type=jnp.float32)
    grad_tokens = lax.psum_scatter(
        dx.astype(jnp.bfloat16), AXES, scatter_dimension=0, tiled=True
    )
    grad_up = lax.dot_general(x_all, up_grad, tn, preferred_element_type=jnp.float32)
    grad_down = lax.dot_general(hidden, row_grad, tn, preferred_element_type=jnp.float32)
    grad_gates = jnp.sum(onehot * dots_home[:, None, :], -1)
    return (
        mixed,
        grad_tokens,
        grad_gates,
        grad_up.astype(jnp.bfloat16)[None],
        grad_down.astype(jnp.bfloat16)[None],
    )


def solution(mesh):
    rows = P(("groups", "expert", "cuts"), None)
    in_specs = (rows,) * 5 + (P("expert", None, "cuts"), P("expert", None, "cuts"), P("expert", "cuts", None))
    out_specs = (rows,) * 3 + (
        P(("groups", "expert"), None, "cuts"),
        P(("groups", "expert"), "cuts", None),
    )
    return jax.shard_map(local, mesh=mesh, in_specs=in_specs, out_specs=out_specs, check_vma=False)
```

time: 251 us -> 312 us (1.24)
  the two profiles are of different devices: /device:TPU:15 before, /device:TPU:0 now
where the time goes in v1:
time: 312 us
  waiting for transfers between devices  209 us (67%)
  matrix products  58.9 us (19%)
  blocking collectives  19.8 us (6%)
  between operations  13.9 us (4%)
  other arithmetic  7.04 us (2%)
    reduce_scatter x1, waiting for transfers between devices, local(): lax.psum_scatter(dx.astype(jnp.bfloat16), AXES, scatter_dimension=0, tile...  63.7 us
    reduce_scatter x1, waiting for transfers between devices, local(): lax.psum_scatter(jnp.where(mine, dots, 0.0), AXES, scatter_dimension=0, t...  53.7 us
    all_gather x1, waiting for transfers between devices, local(): x_all = lax.all_gather(inputs, AXES, axis=0, tiled=True)  43.7 us
    all_gather x1, waiting for transfers between devices, local(): cot_all = lax.all_gather(cotangent, AXES, axis=0, tiled=True)  26.4 us
    reduce_scatter x1, waiting for transfers between devices, local(): lax.psum_scatter((weight * out).astype(jnp.bfloat16), AXES, scatter_dimen...  20.7 us
    all_gather x1, blocking collectives, local(): weight_all = lax.all_gather(weight_of, AXES, axis=0, tiled=True)  19.8 us
    dot_general x1, matrix products, local(): out = jnp.dot(hidden, wd, preferred_element_type=jnp.float32)  8.51 us
    dot_general x1, matrix products, local(): lax.dot_general(row_grad, wd, nt, preferred_element_type=jnp.float32)  8.42 us
  transfers between devices with their start and end apart: 5, of which 5 were waited for; matrix products, arithmetic and copies ran while one was open for 16% of the time, Pallas kernels for 0%

profile of v1, /device:TPU:0, one launch (start us, length us, event | category | flops | bytes accessed | tf_op | source)
XLA Modules:
  0.0 311.6 jit_solution(5513206760478249977)
XLA Ops:
  7.2 0.0 all-gather.3.cloned.1.call-start
  7.2 0.8 mul.68
  8.0 1.7 fusion.26
  9.7 0.0 all-gather.3.cloned.1.call-update
  9.7 0.0 all-gather.5.cloned.1.call-start
  9.8 0.7 all-gather.5.cloned.1.call-update
  10.5 0.0 reduce-scatter.8.cloned.1.call-start
  10.6 43.7 %all-gather.3.cloned.1.call-done = bf16[256,3584]{1,0:T(8,128)(2,1)} async-done(((bf16[16,3584]{1,0:T(8,128)(2,1)}), bf16[256,3584]{1,0:T(8,128)(2,1)}) %all-gather.3.cloned.1.call-update) | async-done | bytes 1835024 | tf_op jit(solution)/shard_map/all_gather | solution.py:26
  54.2 0.0 copy-start
  54.2 6.8 %fusion.12 = f32[256,1280]{1,0:T(8,128)S(1)} fusion(bf16[256,3584]{1,0:T(8,128)(2,1)} %all-gather.3.cloned.1.call-done, bf16[1,3584,1280]{2,1,0:T(8,128)(2,1)} %param.13), kind=kOutput, calls=%fused_computation.14 | convolution fusion | flops 2348810240 | bytes 12320768 | tf_op jit(solution)/shard_map/dot_general | solution.py:35
  61.0 0.0 copy-start.4
  61.0 1.1 copy-done.4
  62.1 0.0 copy-done
  62.1 7.3 %multiply_convert_fusion.3 = (bf16[256,1280]{1,0:T(8,128)(2,1)S(1)}, f32[256,1280]{1,0:T(8,128)}) fusion(f32[256,1280]{1,0:T(8,128)S(1)} %fusion.12, bf16[256,3584]{1,0:T(8,128)(2,1)S(1)} %copy-done, bf16[1,3584,1280]{2,1,0:T(8,128)(2,1)} %param.14), kind=kOutput, calls=%fused_computation.25 | convolution fusion | flops 2350776320 | bytes 14286848 | tf_op jit(solution)/shard_map/dot_general | solution.py:36
  69.4 26.4 %all-gather.5.cloned.1.call-done = bf16[256,3584]{1,0:T(8,128)(2,1)} async-done(((bf16[16,3584]{1,0:T(8,128)(2,1)}), bf16[256,3584]{1,0:T(8,128)(2,1)}) %all-gather.5.cloned.1.call-update) | async-done | bytes 1835024 | tf_op jit(solution)/shard_map/all_gather | solution.py:28
  95.8 0.0 copy-start.2
  95.8 0.0 copy-start.3
  95.8 8.5 %fusion.21 = (f32[256]{0:T(256)S(1)}, f32[256,3584]{1,0:T(8,128)}) fusion(bf16[256,3584]{1,0:T(8,128)(2,1)} %all-gather.5.cloned.1.call-done, bf16[256,1280]{1,0:T(8,128)(2,1)S(1)} %get-tuple-element.12, bf16[1,1280,3584]{2,1,0:T(8,128)(2,1)} %param.15), kind=kOutput, calls=%fused_computation.21 | convolution fusion | flops 2351562496 | bytes 15336448 | tf_op jit(solution)/shard_map/dot_general | solution.py:40
  104.3 0.7 broadcast_select_fusion
  105.1 0.0 reduce-scatter.8.cloned.1.call-update
  105.1 0.0 reduce-scatter.4.cloned.1.call-start
  105.1 0.0 copy-done.2
  105.1 0.1 copy.17
  105.2 0.0 copy-done.3
  105.2 0.1 copy.18
  105.3 53.7 %reduce-scatter.8.cloned.1.call-done = f32[16,16]{1,0:T(8,128)} async-done(((f32[256,16]{1,0:T(8,128)}), f32[16,16]{1,0:T(8,128)}) %reduce-scatter.8.cloned.1.call-update) | async-done | bytes 1040 | tf_op jit(solution)/shard_map/reduce_scatter | solution.py:45
  159.0 0.9 select_reduce_fusion.1
  159.9 19.8 %all_gather.9 = f32[256,16]{1,0:T(8,128)S(1)} all-gather(f32[16,16]{1,0:T(8,128)S(1)} %get-tuple-element.11), channel_id=1, replica_groups=mesh['groups'=2,'expert'=16,'cuts'=1] {'expert','cuts'}, dimensions={0}, use_global_device_ids=true | all-gather | bytes 17408 | tf_op jit(solution)/shard_map/all_gather | solution.py:27
  179.7 0.1 select_reduce_fusion
  179.8 3.6 %multiply_convert_fusion = bf16[256,3584]{1,0:T(8,128)(2,1)} fusion(f32[256,3584]{1,0:T(8,128)} %get-tuple-element.15, f32[256]{0:T(256)S(1)} %select_reduce_fusion), kind=kLoop, calls=%fused_computation.22 | loop fusion | flops 1835008 | bytes 5506048 | tf_op jit(solution)/shard_map/convert_element_type | solution.py:43
  183.4 0.0 reduce-scatter.4.cloned.1.call-update
  183.4 0.2 reduce-scatter.6.cloned.1.call-start
  183.7 0.0 slice-start
  183.7 0.0 slice-start.1
  183.7 8.4 %multiply_convert_fusion.1 = (bf16[256,1280]{1,0:T(8,128)(2,1)S(1)}, f32[256,1280]{1,0:T(8,128)}) fusion(f32[256,1280]{1,0:T(8,128)} %copy-done.4, bf16[1,1280,3584]{2,1,0:T(8,128)(2,1)} %param.15, bf16[256,3584]{1,0:T(8,128)(2,1)} %all-gather.5.cloned.1.call-done, f32[256]{0:T(256)S(1)} %select_reduce_fusion), kind=kOutput, calls=%fused_computation.23 | convolution fusion | flops 2353528832 | bytes 14287872 | tf_op jit(solution)/shard_map/dot_general | solution.py:50
  192.1 0.0 slice-start.2
  192.1 0.0 copy-start.5
  192.1 8.4 %fusion.6 = f32[256,3584]{1,0:T(8,128)} fusion(bf16[256,1280]{1,0:T(8,128)(2,1)S(1)} %get-tuple-element.16, bf16[1,3584,1280]{2,1,0:T(8,128)(2,1)} %param.14), kind=kOutput, calls=%fused_computation.8 | convolution fusion | flops 2348810240 | bytes 13500416 | tf_op jit(solution)/shard_map/dot_general | solution.py:54
  200.5 0.0 slice-done
  200.5 0.0 slice-done.1
  200.5 0.0 slice-done.2
  200.5 0.0 copy-done.5
  200.5 6.8 %fusion.17 = bf16[256,3584]{1,0:T(8,128)(2,1)} fusion(f32[256,3584]{1,0:T(8,128)} %fusion.6, bf16[1,3584,1280]{2,1,0:T(8,128)(2,1)S(1)} %bitcast.43, f32[256,1280]{1,0:T(8,128)S(1)} %copy-done.5, f32[256,1280]{1,0:T(8,128)} %get-tuple-element.17, f32[256,1280]{1,0:T(8,128)} %get-tuple-element.13), kind=kOutput, calls=%fused_computation.17 | convolution fusion | flops 2353922048 | bytes 18612224 | tf_op jit(solution)/shard_map/dot_general | solution.py:53
  207.4 0.0 reduce-scatter.6.cloned.1.call-update
  207.4 0.7 copy.20
  208.1 0.0 copy-start.1
  208.1 6.3 %fusion = bf16[1,3584,1280]{2,1,0:T(8,128)(2,1)} fusion(bf16[256,3584]{1,0:T(8,128)(2,1)S(1)} %copy-done, bf16[256,1280]{1,0:T(8,128)(2,1)S(1)} %get-tuple-element.16), kind=kOutput, calls=%fused_computation.2 | convolution fusion | flops 2353397760 | bytes 11665408 | tf_op jit(solution)/shard_map/dot_general | solution.py:58
  214.3 0.0 copy-done.1
  214.3 6.3 %fusion.1 = bf16[1,1280,3584]{2,1,0:T(8,128)(2,1)} fusion(bf16[256,1280]{1,0:T(8,128)(2,1)S(1)} %get-tuple-element.12, bf16[256,3584]{1,0:T(8,128)(2,1)S(1)} %copy-done.1, f32[256]{0:T(256)S(1)} %select_reduce_fusion), kind=kOutput, calls=%fused_computation.3 | convolution fusion | flops 2356150272 | bytes 11666432 | tf_op jit(solution)/shard_map/dot_general | solution.py:59
  220.7 20.7 %reduce-scatter.4.cloned.1.call-done = bf16[16,3584]{1,0:T(8,128)(2,1)} async-done(((bf16[256,3584]{1,0:T(8,128)(2,1)}), bf16[16,3584]{1,0:T(8,128)(2,1)}) %reduce-scatter.4.cloned.1.call-update) | async-done | bytes 114704 | tf_op jit(solution)/shard_map/reduce_scatter | solution.py:42
  241.4 63.7 %reduce-scatter.6.cloned.1.call-done = bf16[16,3584]{1,0:T(8,128)(2,1)} async-done(((bf16[256,3584]{1,0:T(8,128)(2,1)}), bf16[16,3584]{1,0:T(8,128)(2,1)}) %reduce-scatter.6.cloned.1.call-update) | async-done | bytes 114704 | tf_op jit(solution)/shard_map/reduce_scatter | solution.py:55
  (2 shorter events, 0.0 us)
Async XLA Ops:
  7.2 47.0 %all-gather.3.cloned.1.call-start = ((), (), s32[]{:S(2)}) async-start(), calls=%async_computation.3 | async-start | bytes 1949696 | tf_op jit(solution)/shard_map/all_gather | solution.py:26
  9.7 86.1 %all-gather.5.cloned.1.call-start = ((), (), s32[]{:S(2)}) async-start(), calls=%async_computation.5 | async-start | bytes 1949696 | tf_op jit(solution)/shard_map/all_gather | solution.py:28
  10.5 148.5 %reduce-scatter.8.cloned.1.call-start = ((), (), s32[]{:S(2)}) async-start(), calls=%async_computation.7 | async-start | bytes 139264 | tf_op jit(solution)/shard_map/reduce_scatter | solution.py:45
  54.2 7.9 %copy-start = (bf16[256,3584]{1,0:T(8,128)(2,1)S(1)}, bf16[256,3584]{1,0:T(8,128)(2,1)}, u32[]{:S(2)}) copy-start(bf16[256,3584]{1,0:T(8,128)(2,1)} %all-gather.3.cloned.1.call-done) | copy-start | bytes 5505028
  61.0 1.1 copy-start.4
  95.8 9.3 %copy-start.2 = (s32[16,8]{0,1:T(8,128)S(1)}, s32[16,8]{0,1:T(8,128)}, u32[]{:S(2)}) copy-start(s32[16,8]{0,1:T(8,128)} %param.10) | copy-start | bytes 1540
  95.8 9.4 %copy-start.3 = (f32[16,8]{0,1:T(8,128)S(1)}, f32[16,8]{0,1:T(8,128)}, u32[]{:S(2)}) copy-start(f32[16,8]{0,1:T(8,128)} %param.11) | copy-start | bytes 1540
  105.1 136.3 %reduce-scatter.4.cloned.1.call-start = ((), (), s32[]{:S(2)}) async-start(), calls=%async_computation.4 | async-start | bytes 1949696 | tf_op jit(solution)/shard_map/reduce_scatter | solution.py:42
  183.4 121.6 %reduce-scatter.6.cloned.1.call-start = ((), (), s32[]{:S(2)}) async-start(), calls=%async_computation.6 | async-start | bytes 1949696 | tf_op jit(solution)/shard_map/reduce_scatter | solution.py:55
  183.7 16.8 %slice-start = ((s8[9175040]{0:T(1024)(128)(4,1)}), s8[4194304]{0:T(1024)(128)(4,1)S(1)}, s32[]{:S(2)}) async-start(s8[9175040]{0:T(1024)(128)(4,1)} %bitcast.42), calls=%async_computation.8 | async-start | bytes 8388608
  183.7 16.8 %slice-start.1 = ((s8[9175040]{0:T(1024)(128)(4,1)}), s8[4194304]{0:T(1024)(128)(4,1)S(1)}, s32[]{:S(2)}) async-start(s8[9175040]{0:T(1024)(128)(4,1)} %bitcast.42), calls=%async_computation.9 | async-start | bytes 8388608
  192.1 8.4 %slice-start.2 = ((s8[9175040]{0:T(1024)(128)(4,1)}), s8[786432]{0:T(1024)(128)(4,1)S(1)}, s32[]{:S(2)}) async-start(s8[9175040]{0:T(1024)(128)(4,1)} %bitcast.42), calls=%async_computation.10 | async-start | bytes 1572864
  192.1 8.4 %copy-start.5 = (f32[256,1280]{1,0:T(8,128)S(1)}, f32[256,1280]{1,0:T(8,128)}, u32[]{:S(2)}) copy-start(f32[256,1280]{1,0:T(8,128)} %copy-done.4) | copy-start | bytes 3932164
  208.1 6.3 %copy-start.1 = (bf16[256,3584]{1,0:T(8,128)(2,1)S(1)}, bf16[256,3584]{1,0:T(8,128)(2,1)}, u32[]{:S(2)}) copy-start(bf16[256,3584]{1,0:T(8,128)(2,1)} %all-gather.5.cloned.1.call-done) | copy-start | bytes 5505028
Sparse Core Ops, SparseCore 0:
  10.9 43.3 all-gather.2
  56.5 39.2 all-gather.4
  105.2 53.7 reduce-scatter.7
  183.6 57.7 reduce-scatter.3
  245.5 59.5 reduce-scatter.5

commit v2 on v1

v2 whole, which is shorter than its diff:
```python
import functools

import jax
import jax.numpy as jnp
from jax import lax
from jax.experimental import pallas as pl
from jax.experimental.pallas import tpu as pltpu
from jax.sharding import PartitionSpec as P

MESH = pl.DeviceIdType.MESH
LANES = 128
NT = (((1,), (1,)), ((), ()))
TN = (((0,), (0,)), ((), ()))
F32 = jnp.float32
BF16 = jnp.bfloat16


def parts_of(value):
    high = value.astype(BF16)
    rest = value - high.astype(F32)
    middle = rest.astype(BF16)
    return high, middle, (rest - middle.astype(F32)).astype(BF16)


def kernel(
    experts, cuts, quant, scales, routes, gates, cot, wg_hbm, wu_hbm, wd_hbm,
    mixed, grad_tokens, grad_gates, x_out, up_out, hidden_out, row_out,
    xg, cg, wg, wu, wd, rg, hidden, gate_grad, up_grad, slope, act, weight, dot_acc,
    mix_part, dx_part, sib_mix, sib_dx, out_r, in_r, out_l, in_l,
    w_sem, o_sem, gs_sem, gr_sem, rs_sem, rr_sem,
):
    devices = experts * cuts
    ring = devices // 2
    hops_r = ring // 2
    hops_l = ring - 1 - hops_r
    count, width = quant.shape
    rows = devices * count
    hid = wg.shape[1]
    tile = 256 if hid % 256 == 0 else 128
    col = 256
    half = width // 2

    expert = lax.axis_index("expert")
    me = expert * cuts + lax.axis_index("cuts")
    core = lax.rem(me, 2)
    chip = me // 2

    def chip_at(p):
        if cuts > 1:
            return p
        upper = p // hops_r
        return upper * (2 * (ring - 1 - p) + 1) + (1 - upper) * 2 * p

    if cuts > 1:
        pos = chip
    else:
        y = lax.rem(chip, 2)
        z = chip // 2
        pos = z + y * (ring - 1 - 2 * z)

    def wrap(p):
        return lax.rem(p + 2 * ring, ring)

    def device(p, c):
        i = chip_at(p) * 2 + c
        return {"expert": i // cuts, "cuts": lax.rem(i, cuts)}

    right = device(wrap(pos + 1), core)
    left = device(wrap(pos - 1), core)
    sibling = device(pos, 1 - core)

    loads = [
        pltpu.make_async_copy(src.at[0], dst, w_sem.at[n])
        for n, (src, dst) in enumerate(((wg_hbm, wg), (wu_hbm, wu), (wd_hbm, wd)))
    ]
    for load in loads:
        load.start()

    own = core * ring + pos
    for b in range(scales.shape[1]):
        block = pl.ds(b * (width // scales.shape[1]), width // scales.shape[1])
        xg[own, :, block] = (
            quant[:, block].astype(F32) * scales[:, b : b + 1].astype(F32)
        ).astype(BF16)
    lane = lax.broadcasted_iota(jnp.int32, (count, LANES), 1)
    pay = jnp.zeros((count, LANES), F32)
    for k in range(routes.shape[1]):
        pay += jnp.where(lane == routes[:, k : k + 1], gates[:, k : k + 1], 0.0)
    cg[own, :, 0:width] = cot[...]
    packed = jnp.zeros((count, LANES), F32)
    for n, part in enumerate(parts_of(pay)):
        part = part.astype(F32)
        shifted = part if n == 0 else pltpu.roll(part, n * experts, 1)
        packed += shifted
    cg[own, :, width : width + LANES] = packed.astype(BF16)

    barrier = pltpu.get_barrier_semaphore()
    for other in (left, right, sibling):
        pl.semaphore_signal(barrier, inc=1, device_id=other, device_id_type=MESH)
    pl.semaphore_wait(barrier, 3)

    sends = []

    def gather(which, buf):
        def move(p, c, n, to):
            ref = buf.at[c * ring + p]
            return pltpu.make_async_remote_copy(
                src_ref=ref, dst_ref=ref, send_sem=gs_sem.at[which, n],
                recv_sem=gr_sem.at[which, n], device_id=to, device_id_type=MESH,
            )

        def go(p, n, to):
            copy = move(p, core, n, to)
            copy.start()
            sends.append(copy)

        def step(s):
            if s == 0:
                go(pos, 0, right)
                go(pos, hops_r, left)
                go(pos, ring, sibling)
                return
            if s - 1 < hops_r:
                p = wrap(pos - s)
                move(p, core, s - 1, right).wait_recv()
                if s < hops_r:
                    go(p, s, right)
                go(p, ring + s, sibling)
            if s - 1 < hops_l:
                p = wrap(pos + s)
                move(p, core, hops_r + s - 1, left).wait_recv()
                if s < hops_l:
                    go(p, hops_r + s, left)
                go(p, ring + hops_r + s, sibling)

        def finish():
            for k in range(ring):
                p = pos - k if k <= hops_r else pos + (k - hops_r)
                move(wrap(p), 1 - core, ring + k, sibling).wait_recv()

        return step, finish

    x_step, x_finish = gather(0, xg)
    c_step, c_finish = gather(1, cg)
    lag = 2
    for s in range(hops_r + 1):
        x_step(s)
        if s >= lag:
            c_step(s - lag)
    x_finish()
    outs = []

    def store(n, src, dst):
        copy = pltpu.make_async_copy(src, dst, o_sem.at[n])
        copy.start()
        outs.append(copy)

    store(0, xg, x_out)

    def up_tiles(first, last):
        @pl.loop(first, last)
        def _(n):
            cols = pl.ds(pl.multiple_of(n * tile, tile), tile)
            x = xg[...].reshape(rows, width)
            gate = jnp.dot(x, wg[:, cols], preferred_element_type=F32)
            up = jnp.dot(x, wu[:, cols], preferred_element_type=F32)
            sig = jax.nn.sigmoid(gate)
            active = gate * sig
            act[:, cols] = active
            slope[:, cols] = up * sig * (1.0 + gate * (1.0 - sig))
            hidden[:, cols] = (active * up).astype(BF16)

    loads[0].wait()
    loads[1].wait()
    tiles = hid // tile
    up_tiles(0, 1)
    c_step(hops_r - 1)
    up_tiles(1, 3)
    c_step(hops_r)
    up_tiles(3, tiles)
    c_finish()
    store(1, hidden, hidden_out)

    row_lane = lax.broadcasted_iota(jnp.int32, (rows, LANES), 1)
    mine = (row_lane == expert) | (row_lane == expert + experts)
    mine = mine | (row_lane == expert + 2 * experts)
    got = cg[:, :, width : width + LANES].reshape(rows, LANES).astype(F32)
    weight[...] = jnp.broadcast_to(
        jnp.sum(jnp.where(mine, got, 0.0), 1, keepdims=True), (rows, LANES)
    )
    loads[2].wait()
    dot_acc[...] = jnp.zeros_like(dot_acc)

    def out_tiles(first, last):
        @pl.loop(first, last)
        def _(n):
            cols = pl.ds(pl.multiple_of(n * col, col), col)
            out = jnp.dot(hidden[...], wd[:, cols], preferred_element_type=F32)
            c = cg[:, :, cols].reshape(rows, col).astype(F32)
            w = weight[:, 0:1]
            dot_acc[...] += c * out
            rg[:, cols] = (w * c).astype(BF16)
            mix_part[:, :, cols] = (w * out).astype(BF16).reshape(devices, count, col)

    def reduce(job, buf, sib, lo, wide):
        cols = pl.ds(lo, wide)
        narrow = pl.ds(0, wide)

        def copy(src, dst, n, to):
            return pltpu.make_async_remote_copy(
                src_ref=src, dst_ref=dst, send_sem=rs_sem.at[job, n],
                recv_sem=rr_sem.at[job, n], device_id=to, device_id_type=MESH,
            )

        def swap_cores():
            c = copy(
                buf.at[pl.ds((1 - core) * ring, ring), :, cols], sib, ring, sibling
            )
            c.start()
            sends.append(c)
            return c

        state = {}

        def begin():
            state["sib"] = swap_cores()

        def base(p):
            return buf[core * ring + p, :, cols].astype(F32) + sib[p].astype(F32)

        def ring_copy(s, go_right):
            if go_right:
                return copy(out_r.at[job, s, :, narrow], in_r.at[job, s, :, narrow], s, right)
            return copy(out_l.at[job, s, :, narrow], in_l.at[job, s, :, narrow], hops_r + s, left)

        def hop(s):
            if s == 0:
                state["sib"].wait_recv()
            for go_right, hops, outb, inb in (
                (True, hops_r, out_r, in_r), (False, hops_l, out_l, in_l)
            ):
                if s >= hops:
                    continue
                p = wrap(pos + hops - s) if go_right else wrap(pos - hops + s)
                total = base(p)
                if s > 0:
                    ring_copy(s - 1, go_right).wait_recv()
                    total += inb[job, s - 1, :, narrow].astype(F32)
                outb[job, s, :, narrow] = total.astype(BF16)
                c = ring_copy(s, go_right)
                c.start()
                sends.append(c)

        def last():
            ring_copy(hops_r - 1, True).wait_recv()
            ring_copy(hops_l - 1, False).wait_recv()
            return (
                base(pos)
                + in_r[job, hops_r - 1, :, narrow].astype(F32)
                + in_l[job, hops_l - 1, :, narrow].astype(F32)
            )

        return begin, hop, last

    mix0 = reduce(0, mix_part, sib_mix.at[0, :, :, pl.ds(0, half)], 0, half)
    mix1 = reduce(1, mix_part, sib_mix.at[1], half, half + LANES)
    dx0 = reduce(2, dx_part, sib_dx.at[0], 0, half)
    dx1 = reduce(3, dx_part, sib_dx.at[1], half, half)

    per_half = half // col
    out_tiles(0, per_half)
    mix0[0]()
    out_tiles(per_half, 2 * per_half)
    store(2, rg, row_out)
    dots = jnp.sum(dot_acc[...], 1, keepdims=True)
    extra = jnp.zeros((rows, LANES), F32)
    for n, part in enumerate(parts_of(dots)):
        extra += jnp.where(row_lane == me + n * devices, part.astype(F32), 0.0)
    mix_part[:, :, width : width + LANES] = extra.astype(BF16).reshape(devices, count, LANES)
    mix1[0]()
    mix0[1](0)

    @pl.loop(0, tiles)
    def _(n):
        cols = pl.ds(pl.multiple_of(n * tile, tile), tile)
        grad = lax.dot_general(rg[...], wd[cols, :], NT, preferred_element_type=F32)
        gate_grad[:, cols] = (grad * slope[:, cols]).astype(BF16)
        up_grad[:, cols] = (grad * act[:, cols]).astype(BF16)

    store(3, up_grad, up_out)
    mix1[1](0)
    mix0[1](1)

    def dx_tiles(first, last):
        @pl.loop(first, last)
        def _(n):
            cols = pl.ds(pl.multiple_of(n * col, col), col)
            dx = lax.dot_general(gate_grad[...], wg[cols, :], NT, preferred_element_type=F32)
            dx += lax.dot_general(up_grad[...], wu[cols, :], NT, preferred_element_type=F32)
            dx_part[:, :, cols] = dx.astype(BF16).reshape(devices, count, col)

    mid = per_half // 2
    dx_tiles(0, mid)
    mix1[1](1)
    mix0[1](2)
    dx_tiles(mid, per_half)
    dx0[0]()
    mix1[1](2)
    mix0[1](3)
    dx_tiles(per_half, per_half + mid)
    dx0[1](0)
    mix1[1](3)
    dx_tiles(per_half + mid, 2 * per_half)
    dx1[0]()
    for s in range(4, hops_r):
        mix0[1](s)
        mix1[1](s)
    for s in range(1, hops_r):
        dx0[1](s)
        dx1[1](s - 1)
    dx1[1](hops_r - 1)

    mixed[:, 0:half] = mix0[2]().astype(BF16)
    rest = mix1[2]()
    mixed[:, half:width] = rest[:, 0:half].astype(BF16)
    sums = rest[:, half : half + LANES]
    slot = lax.broadcasted_iota(jnp.int32, (count, routes.shape[1]), 1)
    found = jnp.zeros((count, routes.shape[1]), F32)
    for k in range(routes.shape[1]):
        base_lane = routes[:, k : k + 1] * cuts
        picked = lane < 0
        for n in range(3):
            for c in range(cuts):
                picked = picked | (lane == base_lane + (c + n * devices))
        value = jnp.sum(jnp.where(picked, sums, 0.0), 1, keepdims=True)
        found += jnp.where(slot == k, value, 0.0)
    grad_gates[...] = found
    grad_tokens[:, 0:half] = dx0[2]().astype(BF16)
    grad_tokens[:, half:width] = dx1[2]().astype(BF16)

    for copy in sends:
        copy.wait_send()
    for copy in outs:
        copy.wait()


def local(quant, scales, routes, gates, cotangent, w_gate, w_up, w_down):
    cuts = lax.axis_size("cuts")
    experts = lax.axis_size("expert")
    devices = experts * cuts
    ring = devices // 2
    hops_r = ring // 2
    hops_l = ring - 1 - hops_r
    count, width = quant.shape
    hid = w_gate.shape[2]
    rows = devices * count
    half = width // 2
    vmem = pl.BlockSpec(memory_space=pltpu.VMEM)
    hbm = pl.BlockSpec(memory_space=pl.ANY)
    sds = jax.ShapeDtypeStruct
    dma = pltpu.SemaphoreType.DMA
    mixed, grad_tokens, grad_gates, x_all, up_grad, hidden, row_grad = pl.pallas_call(
        functools.partial(kernel, experts, cuts),
        out_shape=(
            sds((count, width), BF16),
            sds((count, width), BF16),
            sds(gates.shape, F32),
            sds((devices, count, width), BF16),
            sds((rows, hid), BF16),
            sds((rows, hid), BF16),
            sds((rows, width), BF16),
        ),
        in_specs=[vmem] * 5 + [hbm] * 3,
        out_specs=(vmem,) * 3 + (hbm,) * 4,
        scratch_shapes=[
            pltpu.VMEM((devices, count, width), BF16),
            pltpu.VMEM((devices, count, width + LANES), BF16),
            pltpu.VMEM((width, hid), BF16),
            pltpu.VMEM((width, hid), BF16),
            pltpu.VMEM((hid, width), BF16),
            pltpu.VMEM((rows, width), BF16),
            pltpu.VMEM((rows, hid), BF16),
            pltpu.VMEM((rows, hid), BF16),
            pltpu.VMEM((rows, hid), BF16),
            pltpu.VMEM((rows, hid), F32),
            pltpu.VMEM((rows, hid), F32),
            pltpu.VMEM((rows, LANES), F32),
            pltpu.VMEM((rows, 256), F32),
            pltpu.VMEM((devices, count, width + LANES), BF16),
            pltpu.VMEM((devices, count, width), BF16),
            pltpu.VMEM((2, ring, count, half + LANES), BF16),
            pltpu.VMEM((2, ring, count, half), BF16),
            pltpu.VMEM((4, hops_r, count, half + LANES), BF16),
            pltpu.VMEM((4, hops_r, count, half + LANES), BF16),
            pltpu.VMEM((4, hops_l, count, half + LANES), BF16),
            pltpu.VMEM((4, hops_l, count, half + LANES), BF16),
            dma((3,)),
            dma((4,)),
            dma((2, 2 * ring)),
            dma((2, 2 * ring)),
            dma((4, ring + 1)),
            dma((4, ring + 1)),
        ],
        compiler_params=pltpu.CompilerParams(
            collective_id=0, has_side_effects=True, vmem_limit_bytes=60 * 1024 * 1024
        ),
        cost_estimate=pl.CostEstimate(
            flops=12 * rows * width * hid,
            bytes_accessed=6 * width * hid + 4 * rows * (width + hid),
            transcendentals=rows * hid,
        ),
    )(quant, scales, routes, gates, cotangent, w_gate, w_up, w_down)
    x_all = x_all.reshape(rows, width)
    grad_up = lax.dot_general(x_all, up_grad, TN, preferred_element_type=F32)
    grad_down = lax.dot_general(hidden, row_grad, TN, preferred_element_type=F32)
    return (
        mixed,
        grad_tokens,
        grad_gates,
        grad_up.astype(BF16)[None],
        grad_down.astype(BF16)[None],
    )


def solution(mesh):
    rows = P(("groups", "expert", "cuts"), None)
    in_specs = (rows,) * 5 + (
        P("expert", None, "cuts"),
        P("expert", None, "cuts"),
        P("expert", "cuts", None),
    )
    out_specs = (rows,) * 3 + (
        P(("groups", "expert"), None, "cuts"),
        P(("groups", "expert"), "cuts", None),
    )
    return jax.shard_map(local, mesh=mesh, in_specs=in_specs, out_specs=out_specs, check_vma=False)
```

time: 312 us -> 96 us (0.31)
  waiting for transfers between devices: 209 us -> 0 us
  Pallas kernels: 0 us -> 75.4 us
  matrix products: 58.9 us -> 14.2 us
  blocking collectives: 19.8 us -> 0 us
  between operations: 13.9 us -> 0.66 us
  other arithmetic: 7.04 us -> 0 us
    reduce_scatter x3 -> x0, waiting for transfers between devices: 138 us -> none  [the longest x1 63.7 us: local(): lax.psum_scatter(dx.astype(jnp.bfloat16), AXES, scatter_dimension=0, tile...]
    pallas_call x0 -> x1, Pallas kernels: none -> 75.4 us  [local(): pl.pallas_call(functools.partial(kernel, experts, cuts), out_shape=(sds((...]
    all_gather x2 -> x0, waiting for transfers between devices: 70.1 us -> none  [the longest x1 43.7 us: local(): x_all = lax.all_gather(inputs, AXES, axis=0, tiled=True)]
    dot_general x8 -> x2, matrix products: 58.9 us -> 14.2 us  [the longest x1 7.94 us: local(): grad_up = lax.dot_general(x_all, up_grad, TN, preferred_element_type=F32)]
    all_gather x1 -> x0, blocking collectives: 19.8 us -> none  [local(): weight_all = lax.all_gather(weight_of, AXES, axis=0, tiled=True)]
    convert_element_type x2 -> x0, other arithmetic: 5.33 us -> none  [the longest x1 3.65 us: local(): (weight * out).astype(jnp.bfloat16)]
    unnamed x21 -> x13, local copies, waits for them, and re-layouts: 1.91 us -> 5.53 us
  transfers between devices with their start and end apart: 5 -> 0, of which waited for: 5 -> 0; matrix products, arithmetic and copies ran while one was open for 16% -> 0% of each run, Pallas kernels for 0% -> 0%
where the time goes in v2:
time: 96 us; the launch traced here: 95.8 us
  Pallas kernels  75.4 us (79%)
  matrix products  14.2 us (15%)
  local copies, waits for them, and re-layouts  5.53 us (6%)
    pallas_call x1, Pallas kernels, local(): pl.pallas_call(functools.partial(kernel, experts, cuts), out_shape=(sds((...  75.4 us
    dot_general x1, matrix products, local(): grad_up = lax.dot_general(x_all, up_grad, TN, preferred_element_type=F32)  7.94 us
    dot_general x1, matrix products, local(): lax.dot_general(hidden, row_grad, TN, preferred_element_type=F32)  6.24 us
    unnamed x13, local copies, waits for them, and re-layouts  5.53 us

profile of v2, /device:TPU:0, one launch (start us, length us, event | category | flops | bytes accessed | tf_op | source)
XLA Modules:
  0.0 95.8 jit_solution(11573816088387552289)
XLA Ops:
  0.6 1.4 %copy.13.routes = s32[16,8]{1,0:T(8,128)} copy(s32[16,8]{0,1:T(8,128)} %param.10) | data formatting | bytes 1024 | tf_op args[2]
  2.0 1.4 %copy.14.gates = f32[16,8]{1,0:T(8,128)} copy(f32[16,8]{0,1:T(8,128)} %param.11) | data formatting | bytes 1024 | tf_op args[3]
  3.3 75.4 %shard_map.119 = (bf16[16,3584]{1,0:T(8,128)(2,1)}, bf16[16,3584]{1,0:T(8,128)(2,1)}, f32[16,8]{1,0:T(8,128)}, bf16[16,16,3584]{2,1,0:T(8,128)(2,1)}, bf16[256,1...) custom-call(bf16[16,3584]{1,0:T(8,128)(2,1)} %quant.1, bf16[16,28]{1,0:T(8,128)(2,1)} %scales.1, ...), custom_call_target="tpu_custom_call" | custom-call | flops 14092861440 | bytes 32505856 | tf_op jit(solution)/shard_map/pallas_call | solution.py:362
  78.7 0.0 copy-start
  78.7 0.0 copy-start.1
  78.8 1.5 %copy.15 = f32[16,8]{0,1:T(8,128)} copy(f32[16,8]{1,0:T(8,128)} %get-tuple-element.21) | data formatting | bytes 1024
  80.3 0.0 copy-start.3
  80.3 0.0 copy-start.2
  80.3 7.9 %fusion = bf16[1,3584,1280]{2,1,0:T(8,128)(2,1)} fusion(bf16[256,3584]{1,0:T(8,128)(2,1)} %bitcast.9, bf16[256,1280]{1,0:T(8,128)(2,1)} %get-tuple-element.16), kind=kOutput, calls=%fused_computation.2 | convolution fusion | flops 2353397760 | bytes 11665408 | tf_op jit(solution)/shard_map/dot_general | solution.py:414
  88.2 0.0 copy-done
  88.2 0.0 copy-done.1
  88.2 6.2 %fusion.1 = bf16[1,1280,3584]{2,1,0:T(8,128)(2,1)} fusion(bf16[256,1280]{1,0:T(8,128)(2,1)S(1)} %copy-done.1, bf16[256,3584]{1,0:T(8,128)(2,1)S(1)} %copy-done), kind=kOutput, calls=%fused_computation.3 | convolution fusion | flops 2353397760 | bytes 11665408 | tf_op jit(solution)/shard_map/dot_general | solution.py:415
  94.5 0.0 copy-done.3
  94.5 0.6 copy.18
  95.1 0.0 copy-done.2
  95.1 0.6 copy.19
Async XLA Ops:
  78.7 9.5 %copy-start = (bf16[256,3584]{1,0:T(8,128)(2,1)S(1)}, bf16[256,3584]{1,0:T(8,128)(2,1)}, u32[]{:S(2)}) copy-start(bf16[256,3584]{1,0:T(8,128)(2,1)} %get-tuple-element.18) | copy-start | bytes 5505028
  78.7 9.5 %copy-start.1 = (bf16[256,1280]{1,0:T(8,128)(2,1)S(1)}, bf16[256,1280]{1,0:T(8,128)(2,1)}, u32[]{:S(2)}) copy-start(bf16[256,1280]{1,0:T(8,128)(2,1)} %get-tuple-element.17) | copy-start | bytes 1966084
  80.3 14.2 %copy-start.3 = (bf16[16,3584]{1,0:T(8,128)(2,1)S(1)}, bf16[16,3584]{1,0:T(8,128)(2,1)}, u32[]{:S(2)}) copy-start(bf16[16,3584]{1,0:T(8,128)(2,1)} %get-tuple-element.29) | copy-start | bytes 344068
  80.3 14.8 %copy-start.2 = (bf16[16,3584]{1,0:T(8,128)(2,1)S(1)}, bf16[16,3584]{1,0:T(8,128)(2,1)}, u32[]{:S(2)}) copy-start(bf16[16,3584]{1,0:T(8,128)(2,1)} %get-tuple-element.30) | copy-start | bytes 344068

commit v3 on v2

--- a/solution.py
+++ b/solution.py
@@ -27,12 +27,10 @@
     mixed, grad_tokens, grad_gates, x_out, up_out, hidden_out, row_out,
     xg, cg, wg, wu, wd, rg, hidden, gate_grad, up_grad, slope, act, weight, dot_acc,
     mix_part, dx_part, sib_mix, sib_dx, out_r, in_r, out_l, in_l,
-    w_sem, o_sem, gs_sem, gr_sem, rs_sem, rr_sem,
+    turn, w_sem, o_sem, gs_sem, gr_sem, rs_sem, rr_sem,
 ):
     devices = experts * cuts
     ring = devices // 2
-    hops_r = ring // 2
-    hops_l = ring - 1 - hops_r
     count, width = quant.shape
     rows = devices * count
     hid = wg.shape[1]
@@ -48,7 +46,7 @@
     def chip_at(p):
         if cuts > 1:
             return p
-        upper = p // hops_r
+        upper = p // (ring // 2)
         return upper * (2 * (ring - 1 - p) + 1) + (1 - upper) * 2 * p
 
     if cuts > 1:
@@ -82,10 +80,15 @@
         xg[own, :, block] = (
             quant[:, block].astype(F32) * scales[:, b : b + 1].astype(F32)
         ).astype(BF16)
+    tops = routes.shape[0]
     lane = lax.broadcasted_iota(jnp.int32, (count, LANES), 1)
-    pay = jnp.zeros((count, LANES), F32)
-    for k in range(routes.shape[1]):
-        pay += jnp.where(lane == routes[:, k : k + 1], gates[:, k : k + 1], 0.0)
+    sub = lax.broadcasted_iota(jnp.int32, (LANES, count), 0)
+    pay_t = jnp.zeros((LANES, count), F32)
+    for k in range(tops):
+        pay_t += jnp.where(sub == routes[k : k + 1, :], gates[k : k + 1, :], 0.0)
+    turn[...] = jnp.zeros_like(turn)
+    turn[:, 0:count] = pay_t
+    pay = turn[...].T[0:count, :]
     cg[own, :, 0:width] = cot[...]
     packed = jnp.zeros((count, LANES), F32)
     for n, part in enumerate(parts_of(pay)):
@@ -100,13 +103,15 @@
     pl.semaphore_wait(barrier, 3)
 
     sends = []
-
-    def gather(which, buf):
+    hops = ring // 2
+    shares = ((hops, ring - 1 - hops), (ring - 1 - hops, hops))
+
+    def gather(job, buf, lo, wide, hops_r, hops_l):
         def move(p, c, n, to):
-            ref = buf.at[c * ring + p]
+            ref = buf.at[c * ring + p, :, pl.ds(lo, wide)]
             return pltpu.make_async_remote_copy(
-                src_ref=ref, dst_ref=ref, send_sem=gs_sem.at[which, n],
-                recv_sem=gr_sem.at[which, n], device_id=to, device_id_type=MESH,
+                src_ref=ref, dst_ref=ref, send_sem=gs_sem.at[job, n],
+                recv_sem=gr_sem.at[job, n], device_id=to, device_id_type=MESH,
             )
 
         def go(p, n, to):
@@ -117,37 +122,44 @@
         def step(s):
             if s == 0:
                 go(pos, 0, right)
-                go(pos, hops_r, left)
-                go(pos, ring, sibling)
+                go(pos, hops, left)
+                go(pos, 2 * hops, sibling)
                 return
-            if s - 1 < hops_r:
+            if s <= hops_r:
                 p = wrap(pos - s)
                 move(p, core, s - 1, right).wait_recv()
                 if s < hops_r:
                     go(p, s, right)
-                go(p, ring + s, sibling)
-            if s - 1 < hops_l:
+                go(p, 2 * hops + s, sibling)
+            if s <= hops_l:
                 p = wrap(pos + s)
-                move(p, core, hops_r + s - 1, left).wait_recv()
+                move(p, core, hops + s - 1, left).wait_recv()
                 if s < hops_l:
-                    go(p, hops_r + s, left)
-                go(p, ring + hops_r + s, sibling)
+                    go(p, hops + s, left)
+                go(p, 3 * hops + s, sibling)
 
         def finish():
-            for k in range(ring):
-                p = pos - k if k <= hops_r else pos + (k - hops_r)
-                move(wrap(p), 1 - core, ring + k, sibling).wait_recv()
+            move(pos, 1 - core, 2 * hops, sibling).wait_recv()
+            for s in range(1, hops_r + 1):
+                move(wrap(pos - s), 1 - core, 2 * hops + s, sibling).wait_recv()
+            for s in range(1, hops_l + 1):
+                move(wrap(pos + s), 1 - core, 3 * hops + s, sibling).wait_recv()
 
         return step, finish
 
-    x_step, x_finish = gather(0, xg)
-    c_step, c_finish = gather(1, cg)
-    lag = 2
-    for s in range(hops_r + 1):
-        x_step(s)
-        if s >= lag:
-            c_step(s - lag)
-    x_finish()
+    x_jobs = [gather(0, xg, 0, half, *shares[0]), gather(1, xg, half, half, *shares[1])]
+    c_jobs = [
+        gather(2, cg, 0, half, *shares[0]),
+        gather(3, cg, half, half + LANES, *shares[1]),
+    ]
+    for s in range(hops + 1):
+        for step, _ in x_jobs:
+            step(s)
+        if s >= 1:
+            for step, _ in c_jobs:
+                step(s - 1)
+    for _, finish in x_jobs:
+        finish()
     outs = []
 
     def store(n, src, dst):
@@ -174,11 +186,11 @@
     loads[1].wait()
     tiles = hid // tile
     up_tiles(0, 1)
-    c_step(hops_r - 1)
-    up_tiles(1, 3)
-    c_step(hops_r)
-    up_tiles(3, tiles)
-    c_finish()
+    for step, _ in c_jobs:
+        step(hops)
+    up_tiles(1, tiles)
+    for _, finish in c_jobs:
+        finish()
     store(1, hidden, hidden_out)
 
     row_lane = lax.broadcasted_iota(jnp.int32, (rows, LANES), 1)
@@ -202,7 +214,7 @@
             rg[:, cols] = (w * c).astype(BF16)
             mix_part[:, :, cols] = (w * out).astype(BF16).reshape(devices, count, col)
 
-    def reduce(job, buf, sib, lo, wide):
+    def reduce(job, buf, sib, lo, wide, hops_r, hops_l):
         cols = pl.ds(lo, wide)
         narrow = pl.ds(0, wide)
 
@@ -214,13 +226,13 @@
 
         def swap_cores():
             c = copy(
-                buf.at[pl.ds((1 - core) * ring, ring), :, cols], sib, ring, sibling
+                buf.at[pl.ds((1 - core) * ring, ring), :, cols], sib, 2 * hops, sibling
             )
             c.start()
             sends.append(c)
             return c
 
-        state = {}
+        state = {"next": 0}
 
         def begin():
             state["sib"] = swap_cores()
@@ -231,17 +243,21 @@
         def ring_copy(s, go_right):
             if go_right:
                 return copy(out_r.at[job, s, :, narrow], in_r.at[job, s, :, narrow], s, right)
-            return copy(out_l.at[job, s, :, narrow], in_l.at[job, s, :, narrow], hops_r + s, left)
-
-        def hop(s):
+            return copy(out_l.at[job, s, :, narrow], in_l.at[job, s, :, narrow], hops + s, left)
+
+        def hop():
+            s = state["next"]
+            if s == hops:
+                return
+            state["next"] = s + 1
             if s == 0:
                 state["sib"].wait_recv()
-            for go_right, hops, outb, inb in (
+            for go_right, most, outb, inb in (
                 (True, hops_r, out_r, in_r), (False, hops_l, out_l, in_l)
             ):
-                if s >= hops:
+                if s >= most:
                     continue
-                p = wrap(pos + hops - s) if go_right else wrap(pos - hops + s)
+                p = wrap(pos + most - s) if go_right else wrap(pos - most + s)
                 total = base(p)
                 if s > 0:
                     ring_copy(s - 1, go_right).wait_recv()
@@ -262,10 +278,10 @@
 
         return begin, hop, last
 
-    mix0 = reduce(0, mix_part, sib_mix.at[0, :, :, pl.ds(0, half)], 0, half)
-    mix1 = reduce(1, mix_part, sib_mix.at[1], half, half + LANES)
-    dx0 = reduce(2, dx_part, sib_dx.at[0], 0, half)
-    dx1 = reduce(3, dx_part, sib_dx.at[1], half, half)
+    mix0 = reduce(0, mix_part, sib_mix.at[0, :, :, pl.ds(0, half)], 0, half, *shares[0])
+    mix1 = reduce(1, mix_part, sib_mix.at[1], half, half + LANES, *shares[1])
+    dx0 = reduce(2, dx_part, sib_dx.at[0], 0, half, *shares[0])
+    dx1 = reduce(3, dx_part, sib_dx.at[1], half, half, *shares[1])
 
     per_half = half // col
     out_tiles(0, per_half)
@@ -278,18 +294,15 @@
         extra += jnp.where(row_lane == me + n * devices, part.astype(F32), 0.0)
     mix_part[:, :, width : width + LANES] = extra.astype(BF16).reshape(devices, count, LANES)
     mix1[0]()
-    mix0[1](0)
-
-    @pl.loop(0, tiles)
-    def _(n):
-        cols = pl.ds(pl.multiple_of(n * tile, tile), tile)
-        grad = lax.dot_general(rg[...], wd[cols, :], NT, preferred_element_type=F32)
-        gate_grad[:, cols] = (grad * slope[:, cols]).astype(BF16)
-        up_grad[:, cols] = (grad * act[:, cols]).astype(BF16)
-
-    store(3, up_grad, up_out)
-    mix1[1](0)
-    mix0[1](1)
+    mix0[1]()
+
+    def hidden_tiles(first, last):
+        @pl.loop(first, last)
+        def _(n):
+            cols = pl.ds(pl.multiple_of(n * tile, tile), tile)
+            grad = lax.dot_general(rg[...], wd[cols, :], NT, preferred_element_type=F32)
+            gate_grad[:, cols] = (grad * slope[:, cols]).astype(BF16)
+            up_grad[:, cols] = (grad * act[:, cols]).astype(BF16)
 
     def dx_tiles(first, last):
         @pl.loop(first, last)
@@ -299,42 +312,45 @@
             dx += lax.dot_general(up_grad[...], wu[cols, :], NT, preferred_element_type=F32)
             dx_part[:, :, cols] = dx.astype(BF16).reshape(devices, count, col)
 
-    mid = per_half // 2
-    dx_tiles(0, mid)
-    mix1[1](1)
-    mix0[1](2)
-    dx_tiles(mid, per_half)
+    hidden_tiles(0, 2)
+    mix1[1]()
+    mix0[1]()
+    hidden_tiles(2, 4)
+    mix1[1]()
+    mix0[1]()
+    hidden_tiles(4, tiles)
+    store(3, up_grad, up_out)
+    dx_tiles(0, 2)
+    mix1[1]()
+    mix0[1]()
+    dx_tiles(2, 5)
+    mix1[1]()
+    dx_tiles(5, per_half)
     dx0[0]()
-    mix1[1](2)
-    mix0[1](3)
-    dx_tiles(per_half, per_half + mid)
-    dx0[1](0)
-    mix1[1](3)
-    dx_tiles(per_half + mid, 2 * per_half)
+    dx_tiles(per_half, per_half + 2)
+    dx0[1]()
+    dx_tiles(per_half + 2, per_half + 5)
+    dx0[1]()
+    dx_tiles(per_half + 5, 2 * per_half)
     dx1[0]()
-    for s in range(4, hops_r):
-        mix0[1](s)
-        mix1[1](s)
-    for s in range(1, hops_r):
-        dx0[1](s)
-        dx1[1](s - 1)
-    dx1[1](hops_r - 1)
+    dx0[1]()
+    for _ in range(hops):
+        for job in (mix0, mix1, dx1, dx0):
+            job[1]()
 
     mixed[:, 0:half] = mix0[2]().astype(BF16)
     rest = mix1[2]()
     mixed[:, half:width] = rest[:, 0:half].astype(BF16)
     sums = rest[:, half : half + LANES]
-    slot = lax.broadcasted_iota(jnp.int32, (count, routes.shape[1]), 1)
-    found = jnp.zeros((count, routes.shape[1]), F32)
-    for k in range(routes.shape[1]):
-        base_lane = routes[:, k : k + 1] * cuts
-        picked = lane < 0
+    turn[0:count, :] = sums
+    sums_t = turn[...].T[:, 0:count]
+    for k in range(tops):
+        base_lane = routes[k : k + 1, :] * cuts
+        picked = sub < 0
         for n in range(3):
             for c in range(cuts):
-                picked = picked | (lane == base_lane + (c + n * devices))
-        value = jnp.sum(jnp.where(picked, sums, 0.0), 1, keepdims=True)
-        found += jnp.where(slot == k, value, 0.0)
-    grad_gates[...] = found
+                picked = picked | (sub == base_lane + (c + n * devices))
+        grad_gates[k : k + 1, :] = jnp.sum(jnp.where(picked, sums_t, 0.0), 0, keepdims=True)
     grad_tokens[:, 0:half] = dx0[2]().astype(BF16)
     grad_tokens[:, half:width] = dx1[2]().astype(BF16)
 
@@ -342,6 +358,19 @@
         copy.wait_send()
     for copy in outs:
         copy.wait()
+
+
+def weight_grads(x, up_grad, hidden, row_grad, grad_up, grad_down, hidden_t):
+    @pl.when(pl.program_id(0) == 0)
+    def _():
+        hidden_t[...] = hidden[...].T
+
+    grad_up[0] = lax.dot_general(
+        x[...], up_grad[...], TN, preferred_element_type=F32
+    ).astype(BF16)
+    grad_down[0] = jnp.dot(
+        hidden_t[...], row_grad[...], preferred_element_type=F32
+    ).astype(BF16)
 
 
 def local(quant, scales, routes, gates, cotangent, w_gate, w_up, w_down):
@@ -349,8 +378,7 @@
     experts = lax.axis_size("expert")
     devices = experts * cuts
     ring = devices // 2
-    hops_r = ring // 2
-    hops_l = ring - 1 - hops_r
+    hops = ring // 2
     count, width = quant.shape
     hid = w_gate.shape[2]
     rows = devices * count
@@ -364,7 +392,7 @@
         out_shape=(
             sds((count, width), BF16),
             sds((count, width), BF16),
-            sds(gates.shape, F32),
+            sds(gates.shape[::-1], F32),
             sds((devices, count, width), BF16),
             sds((rows, hid), BF16),
             sds((rows, hid), BF16),
@@ -390,14 +418,15 @@
             pltpu.VMEM((devices, count, width), BF16),
             pltpu.VMEM((2, ring, count, half + LANES), BF16),
             pltpu.VMEM((2, ring, count, half), BF16),
-            pltpu.VMEM((4, hops_r, count, half + LANES), BF16),
-            pltpu.VMEM((4, hops_r, count, half + LANES), BF16),
-            pltpu.VMEM((4, hops_l, count, half + LANES), BF16),
-            pltpu.VMEM((4, hops_l, count, half + LANES), BF16),
+            pltpu.VMEM((4, hops, count, half + LANES), BF16),
+            pltpu.VMEM((4, hops, count, half + LANES), BF16),
+            pltpu.VMEM((4, hops, count, half + LANES), BF16),
+            pltpu.VMEM((4, hops, count, half + LANES), BF16),
+            pltpu.VMEM((LANES, LANES), F32),
             dma((3,)),
             dma((4,)),
-            dma((2, 2 * ring)),
-            dma((2, 2 * ring)),
+            dma((4, 2 * ring + 1)),
+            dma((4, 2 * ring + 1)),
             dma((4, ring + 1)),
             dma((4, ring + 1)),
         ],
@@ -409,16 +438,37 @@
             bytes_accessed=6 * width * hid + 4 * rows * (width + hid),
             transcendentals=rows * hid,
         ),
-    )(quant, scales, routes, gates, cotangent, w_gate, w_up, w_down)
+    )(quant, scales, routes.T, gates.T, cotangent, w_gate, w_up, w_down)
     x_all = x_all.reshape(rows, width)
-    grad_up = lax.dot_general(x_all, up_grad, TN, preferred_element_type=F32)
-    grad_down = lax.dot_general(hidden, row_grad, TN, preferred_element_type=F32)
+    step = 512
+    grad_up, grad_down = pl.pallas_call(
+        weight_grads,
+        grid=(width // step,),
+        out_shape=(sds((1, width, hid), BF16), sds((1, hid, width), BF16)),
+        in_specs=[
+            pl.BlockSpec((rows, step), lambda n: (0, n)),
+            pl.BlockSpec((rows, hid), lambda n: (0, 0)),
+            pl.BlockSpec((rows, hid), lambda n: (0, 0)),
+            pl.BlockSpec((rows, step), lambda n: (0, n)),
+        ],
+        out_specs=(
+            pl.BlockSpec((1, step, hid), lambda n: (0, n, 0)),
+            pl.BlockSpec((1, hid, step), lambda n: (0, 0, n)),
+        ),
+        scratch_shapes=[pltpu.VMEM((hid, rows), BF16)],
+        compiler_params=pltpu.CompilerParams(vmem_limit_bytes=32 * 1024 * 1024),
+        cost_estimate=pl.CostEstimate(
+            flops=4 * rows * width * hid,
+            bytes_accessed=4 * width * hid + 4 * rows * (width + hid),
+            transcendentals=0,
+        ),
+    )(x_all, up_grad, hidden, row_grad)
     return (
         mixed,
         grad_tokens,
-        grad_gates,
-        grad_up.astype(BF16)[None],
-        grad_down.astype(BF16)[None],
+        grad_gates.T,
+        grad_up,
+        grad_down,
     )
 
 

time: 96 us -> 93.6 us (0.975)
  matrix products: 14.2 us -> 0 us
  Pallas kernels: 75.4 us -> 85.5 us
  local copies, waits for them, and re-layouts: 5.53 us -> 7.06 us
    dot_general x2 -> x0, matrix products: 14.2 us -> none  [the longest x1 7.94 us: local(): grad_up = lax.dot_general(x_all, up_grad, TN, preferred_element_type=F32)]
    pallas_call x0 -> x1, Pallas kernels: none -> 8.41 us  [local(): pl.pallas_call(weight_grads, grid=(width // step,), out_shape=(sds((1, wi...]
    pallas_call x1, Pallas kernels: 75.4 us -> 77.1 us  [local(): pl.pallas_call(functools.partial(kernel, experts, cuts), out_shape=(sds((...]
    unnamed x13 -> x17, local copies, waits for them, and re-layouts: 5.53 us -> 7.06 us
where the time goes in v3:
time: 93.6 us; the launch traced here: 93.3 us
  Pallas kernels  85.5 us (91%)
  local copies, waits for them, and re-layouts  7.06 us (8%)
    pallas_call x1, Pallas kernels, local(): pl.pallas_call(functools.partial(kernel, experts, cuts), out_shape=(sds((...  77.1 us
    pallas_call x1, Pallas kernels, local(): pl.pallas_call(weight_grads, grid=(width // step,), out_shape=(sds((1, wi...  8.41 us
    unnamed x17, local copies, waits for them, and re-layouts  7.06 us

profile of v3, /device:TPU:0, one launch (start us, length us, event | category | flops | bytes accessed | tf_op | source)
XLA Modules:
  0.0 93.3 jit_solution(15978621910192151461)
XLA Ops:
  0.6 77.1 %shard_map.119 = (bf16[16,3584]{1,0:T(8,128)(2,1)}, bf16[16,3584]{1,0:T(8,128)(2,1)}, f32[8,16]{1,0:T(8,128)}, bf16[16,16,3584]{2,1,0:T(8,128)(2,1)}, bf16[256,1...) custom-call(bf16[16,3584]{1,0:T(8,128)(2,1)} %quant.1, bf16[16,28]{1,0:T(8,128)(2,1)} %scales.1, ...), custom_call_target="tpu_custom_call" | custom-call | flops 14092861440 | bytes 32505856 | tf_op jit(solution)/shard_map/pallas_call | solution.py:390
  77.8 0.0 copy-start.6
  77.8 0.0 copy-start
  77.8 1.5 %copy-done = bf16[16,16,3584]{2,1,0:T(8,128)(2,1)S(1)} copy-done((bf16[16,16,3584]{2,1,0:T(8,128)(2,1)S(1)}, bf16[16,16,3584]{2,1,0:T(8,128)(2,1)}, u32[]{:S(2)}) %copy-start) | copy-done | bytes 1835032
  79.3 0.0 copy-start.1
  79.3 1.5 %copy-done.1 = bf16[256,3584]{1,0:T(8,128)(2,1)S(1)} copy-done((bf16[256,3584]{1,0:T(8,128)(2,1)S(1)}, bf16[256,3584]{1,0:T(8,128)(2,1)}, u32[]{:S(2)}) %copy-start.1) | copy-done | bytes 1835032
  80.8 0.0 copy-start.2
  80.8 1.1 %copy-done.2 = bf16[256,1280]{1,0:T(8,128)(2,1)S(1)} copy-done((bf16[256,1280]{1,0:T(8,128)(2,1)S(1)}, bf16[256,1280]{1,0:T(8,128)(2,1)}, u32[]{:S(2)}) %copy-start.2) | copy-done | bytes 655384
  81.9 0.0 copy-start.3
  81.9 1.1 %copy-done.3 = bf16[256,1280]{1,0:T(8,128)(2,1)S(1)} copy-done((bf16[256,1280]{1,0:T(8,128)(2,1)S(1)}, bf16[256,1280]{1,0:T(8,128)(2,1)}, u32[]{:S(2)}) %copy-start.3) | copy-done | bytes 655384
  83.0 0.0 copy-start.5
  83.0 0.0 copy-start.4
  83.0 8.4 %shard_map.120 = (bf16[1,3584,1280]{2,1,0:T(8,128)(2,1)}, bf16[1,1280,3584]{2,1,0:T(8,128)(2,1)}) custom-call(bf16[256,3584]{1,0:T(8,128)(2,1)S(1)} %bitcast.4, bf16[256,1280]{1,0:T(8,128)(2,1)S(1)} %copy-done.2, bf16[256,1280]{1,0:T(8,128)(2,1)S(1)} %copy-done.3, bf16[256,3584]{1,0:T(8,128)(2,1)S(1)} %copy-done.1), custom_call_target="tpu_custom_call" | custom-call | flops 4697620480 | bytes 23330816 | tf_op jit(solution)/shard_map/pallas_call | solution.py:444
  91.4 0.0 copy-done.5
  91.4 0.6 copy.16
  92.0 0.0 copy-done.4
  92.0 0.6 copy.17
  92.7 0.0 copy-done.6
  92.7 0.6 copy.18
Async XLA Ops:
  77.8 14.9 %copy-start.6 = (f32[8,16]{1,0:T(8,128)S(1)}, f32[8,16]{1,0:T(8,128)}, u32[]{:S(2)}) copy-start(f32[8,16]{1,0:T(8,128)} %get-tuple-element.16) | copy-start | bytes 1540
  77.8 1.5 %copy-start = (bf16[16,16,3584]{2,1,0:T(8,128)(2,1)S(1)}, bf16[16,16,3584]{2,1,0:T(8,128)(2,1)}, u32[]{:S(2)}) copy-start(bf16[16,16,3584]{2,1,0:T(8,128)(2,1)} %get-tuple-element.17) | copy-start | bytes 5505028
  79.3 1.5 %copy-start.1 = (bf16[256,3584]{1,0:T(8,128)(2,1)S(1)}, bf16[256,3584]{1,0:T(8,128)(2,1)}, u32[]{:S(2)}) copy-start(bf16[256,3584]{1,0:T(8,128)(2,1)} %get-tuple-element.20.row_grad) | copy-start | bytes 5505028
  80.8 1.1 %copy-start.2 = (bf16[256,1280]{1,0:T(8,128)(2,1)S(1)}, bf16[256,1280]{1,0:T(8,128)(2,1)}, u32[]{:S(2)}) copy-start(bf16[256,1280]{1,0:T(8,128)(2,1)} %get-tuple-element.18.up_grad) | copy-start | bytes 1966084
  81.9 1.1 %copy-start.3 = (bf16[256,1280]{1,0:T(8,128)(2,1)S(1)}, bf16[256,1280]{1,0:T(8,128)(2,1)}, u32[]{:S(2)}) copy-start(bf16[256,1280]{1,0:T(8,128)(2,1)} %get-tuple-element.19.hidden) | copy-start | bytes 1966084
  83.0 8.4 %copy-start.5 = (bf16[16,3584]{1,0:T(8,128)(2,1)S(1)}, bf16[16,3584]{1,0:T(8,128)(2,1)}, u32[]{:S(2)}) copy-start(bf16[16,3584]{1,0:T(8,128)(2,1)} %get-tuple-element.28) | copy-start | bytes 344068
  83.0 9.1 %copy-start.4 = (bf16[16,3584]{1,0:T(8,128)(2,1)S(1)}, bf16[16,3584]{1,0:T(8,128)(2,1)}, u32[]{:S(2)}) copy-start(bf16[16,3584]{1,0:T(8,128)(2,1)} %get-tuple-element.29) | copy-start | bytes 344068

commit v4 on v3

--- a/solution.py
+++ b/solution.py
@@ -27,7 +27,7 @@
     mixed, grad_tokens, grad_gates, x_out, up_out, hidden_out, row_out,
     xg, cg, wg, wu, wd, rg, hidden, gate_grad, up_grad, slope, act, weight, dot_acc,
     mix_part, dx_part, sib_mix, sib_dx, out_r, in_r, out_l, in_l,
-    turn, w_sem, o_sem, gs_sem, gr_sem, rs_sem, rr_sem,
+    turn, x_turned, hidden_turned, w_sem, o_sem, gs_sem, gr_sem, rs_sem, rr_sem,
 ):
     devices = experts * cuts
     ring = devices // 2
@@ -155,9 +155,9 @@
     for s in range(hops + 1):
         for step, _ in x_jobs:
             step(s)
-        if s >= 1:
+        if s < hops:
             for step, _ in c_jobs:
-                step(s - 1)
+                step(s)
     for _, finish in x_jobs:
         finish()
     outs = []
@@ -167,7 +167,6 @@
         copy.start()
         outs.append(copy)
 
-    store(0, xg, x_out)
 
     def up_tiles(first, last):
         @pl.loop(first, last)
@@ -191,7 +190,6 @@
     up_tiles(1, tiles)
     for _, finish in c_jobs:
         finish()
-    store(1, hidden, hidden_out)
 
     row_lane = lax.broadcasted_iota(jnp.int32, (rows, LANES), 1)
     mine = (row_lane == expert) | (row_lane == expert + experts)
@@ -334,9 +332,27 @@
     dx_tiles(per_half + 5, 2 * per_half)
     dx1[0]()
     dx0[1]()
-    for _ in range(hops):
+    def turn_rows(first, last):
+        @pl.loop(first, last)
+        def _(n):
+            cols = pl.ds(pl.multiple_of(n * col, col), col)
+            x_turned[cols, :] = xg[:, :, cols].reshape(rows, col).T
+
+    def turn_hidden(first, last):
+        @pl.loop(first, last)
+        def _(n):
+            cols = pl.ds(pl.multiple_of(n * tile, tile), tile)
+            hidden_turned[cols, :] = hidden[:, cols].T
+
+    turn_hidden(0, tiles)
+    store(1, hidden_turned, hidden_out)
+    for s in range(hops):
         for job in (mix0, mix1, dx1, dx0):
             job[1]()
+        if s < 2:
+            turn_rows(s * per_half, (s + 1) * per_half)
+            if s == 1:
+                store(0, x_turned, x_out)
 
     mixed[:, 0:half] = mix0[2]().astype(BF16)
     rest = mix1[2]()
@@ -360,16 +376,21 @@
         copy.wait()
 
 
-def weight_grads(x, up_grad, hidden, row_grad, grad_up, grad_down, hidden_t):
+def weight_grads(
+    x_turned, up_grad, hidden_turned, row_grad, mixed, grad_tokens, grad_gates,
+    grad_up, grad_down, mixed_out, tokens_out, gates_out,
+):
     @pl.when(pl.program_id(0) == 0)
     def _():
-        hidden_t[...] = hidden[...].T
-
-    grad_up[0] = lax.dot_general(
-        x[...], up_grad[...], TN, preferred_element_type=F32
+        mixed_out[...] = mixed[...]
+        tokens_out[...] = grad_tokens[...]
+        gates_out[...] = grad_gates[...]
+
+    grad_up[0] = jnp.dot(
+        x_turned[...], up_grad[...], preferred_element_type=F32
     ).astype(BF16)
     grad_down[0] = jnp.dot(
-        hidden_t[...], row_grad[...], preferred_element_type=F32
+        hidden_turned[...], row_grad[...], preferred_element_type=F32
     ).astype(BF16)
 
 
@@ -393,9 +414,9 @@
             sds((count, width), BF16),
             sds((count, width), BF16),
             sds(gates.shape[::-1], F32),
-            sds((devices, count, width), BF16),
+            sds((width, rows), BF16),
             sds((rows, hid), BF16),
-            sds((rows, hid), BF16),
+            sds((hid, rows), BF16),
             sds((rows, width), BF16),
         ),
         in_specs=[vmem] * 5 + [hbm] * 3,
@@ -423,6 +444,8 @@
             pltpu.VMEM((4, hops, count, half + LANES), BF16),
             pltpu.VMEM((4, hops, count, half + LANES), BF16),
             pltpu.VMEM((LANES, LANES), F32),
+            pltpu.VMEM((width, rows), BF16),
+            pltpu.VMEM((hid, rows), BF16),
             dma((3,)),
             dma((4,)),
             dma((4, 2 * ring + 1)),
@@ -439,30 +462,40 @@
             transcendentals=rows * hid,
         ),
     )(quant, scales, routes.T, gates.T, cotangent, w_gate, w_up, w_down)
-    x_all = x_all.reshape(rows, width)
     step = 512
-    grad_up, grad_down = pl.pallas_call(
+    small = [
+        pl.BlockSpec(array.shape, lambda n: (0, 0))
+        for array in (mixed, grad_tokens, grad_gates)
+    ]
+    grad_up, grad_down, mixed, grad_tokens, grad_gates = pl.pallas_call(
         weight_grads,
         grid=(width // step,),
-        out_shape=(sds((1, width, hid), BF16), sds((1, hid, width), BF16)),
+        out_shape=(
+            sds((1, width, hid), BF16),
+            sds((1, hid, width), BF16),
+            sds(mixed.shape, BF16),
+            sds(grad_tokens.shape, BF16),
+            sds(grad_gates.shape, F32),
+        ),
         in_specs=[
+            pl.BlockSpec((step, rows), lambda n: (n, 0)),
+            pl.BlockSpec((rows, hid), lambda n: (0, 0)),
+            pl.BlockSpec((hid, rows), lambda n: (0, 0)),
             pl.BlockSpec((rows, step), lambda n: (0, n)),
-            pl.BlockSpec((rows, hid), lambda n: (0, 0)),
-            pl.BlockSpec((rows, hid), lambda n: (0, 0)),
-            pl.BlockSpec((rows, step), lambda n: (0, n)),
+            *small,
         ],
         out_specs=(
             pl.BlockSpec((1, step, hid), lambda n: (0, n, 0)),
             pl.BlockSpec((1, hid, step), lambda n: (0, 0, n)),
+            *small,
         ),
-        scratch_shapes=[pltpu.VMEM((hid, rows), BF16)],
-        compiler_params=pltpu.CompilerParams(vmem_limit_bytes=32 * 1024 * 1024),
+        compiler_params=pltpu.CompilerParams(vmem_limit_bytes=60 * 1024 * 1024),
         cost_estimate=pl.CostEstimate(
             flops=4 * rows * width * hid,
             bytes_accessed=4 * width * hid + 4 * rows * (width + hid),
             transcendentals=0,
         ),
-    )(x_all, up_grad, hidden, row_grad)
+    )(x_all, up_grad, hidden, row_grad, mixed, grad_tokens, grad_gates)
     return (
         mixed,
         grad_tokens,

time: 93.6 us -> 86.9 us (0.928)
  local copies, waits for them, and re-layouts: 7.06 us -> 0 us
    unnamed x17 -> x0, local copies, waits for them, and re-layouts: 7.06 us -> none
    pallas_call x1, Pallas kernels: 8.41 us -> 10.4 us  [local(): pl.pallas_call(weight_grads, grid=(width // step,), out_shape=(sds((1, wi...]
    pallas_call x1, Pallas kernels: 77.1 us -> 75.6 us  [local(): pl.pallas_call(functools.partial(kernel, experts, cuts), out_shape=(sds((...]
where the time goes in v4:
time: 86.9 us; the launch traced here: 86.6 us
  Pallas kernels  86 us (99%)
    pallas_call x1, Pallas kernels, local(): pl.pallas_call(functools.partial(kernel, experts, cuts), out_shape=(sds((...  75.6 us
    pallas_call x1, Pallas kernels, local(): pl.pallas_call(weight_grads, grid=(width // step,), out_shape=(sds((1, wi...  10.4 us

profile of v4, /device:TPU:0, one launch (start us, length us, event | category | flops | bytes accessed | tf_op | source)
XLA Modules:
  0.0 86.6 jit_solution(4375541802414145280)
XLA Ops:
  0.6 75.6 %shard_map.119 = (bf16[16,3584]{1,0:T(8,128)(2,1)}, bf16[16,3584]{1,0:T(8,128)(2,1)}, f32[8,16]{1,0:T(8,128)}, bf16[3584,256]{1,0:T(8,128)(2,1)}, bf16[256,1280]...) custom-call(bf16[16,3584]{1,0:T(8,128)(2,1)} %quant.1, bf16[16,28]{1,0:T(8,128)(2,1)} %scales.1, ...), custom_call_target="tpu_custom_call" | custom-call | flops 14092861440 | bytes 32505856 | tf_op jit(solution)/shard_map/pallas_call | solution.py:411
  76.2 10.4 %shard_map.120 = (bf16[1,3584,1280]{2,1,0:T(8,128)(2,1)}, bf16[1,1280,3584]{2,1,0:T(8,128)(2,1)}, bf16[16,3584]{1,0:T(8,128)(2,1)}, bf16[16,3584]{1,0:T(8,128)(2,1)}, f32[8,16]{1,0:T(8,128)}) custom-call(bf16[3584,256]{1,0:T(8,128)(2,1)} %get-tuple-element.17.x_turned, bf16[256,1280]{1,0:T(8,128)(2,1)} %get-tuple-element.18.up_grad, ...), custom_call_target="tpu_custom_call" | custom-call | flops 4697620480 | bytes 23330816 | tf_op jit(solution)/shard_map/pallas_call | solution.py:470
